TPU v7x, 128 devices: a whole 4x4x4 slice. The times are simulated.
128 devices in a mesh: head: 8 (over z, core), inner: 4 (over x), outer: 4 (over y).
Axes of the slice: x: 4, y: 4, z: 4, core: 2. Of those that a mesh axis runs over, the one named last changes fastest.
Arguments:
- query_in: bfloat16 [32768, 2048], P(('inner', 'outer'), 'head'), may hold values from -6 to 6
- key_in: bfloat16 [32768, 2048], P(('inner', 'outer'), 'head'), may hold values from -5 to 5
- value_in: bfloat16 [32768, 4096], P(('inner', 'outer'), 'head'), may hold values from -6 to 6
- log_decay: float32 [32768, 32], P(('inner', 'outer'), 'head'), may hold values from -1 to 0
- beta_gate: float32 [32768, 32], P(('inner', 'outer'), 'head'), may hold values from 0.6 to 1
- conv_query: bfloat16 [4, 2048], P(None, 'head'), may hold values from -2.5 to 2.5
- conv_key: bfloat16 [4, 2048], P(None, 'head'), may hold values from -2.5 to 2.5
- conv_value: bfloat16 [4, 4096], P(None, 'head'), may hold values from -2.5 to 2.5
- norm_gain: float32 [4096], P('head'), may hold values from 0.25 to 1.75
Outputs:
- layer_out: bfloat16 [32768, 4096], P(('inner', 'outer'), 'head')
All inputs are finite; a program needn't handle non-finite values.
Results may differ from a plain program's by a relative error of at most 0.002.
Values may be sent and summed in bfloat16 or wider, within the bound.
No kernel may reach another device: no remote copies, remote signals or barrier semaphores. Data moves between devices by JAX's collectives and lax.ppermute only.
A program may use at most 128 MiB of HBM per device.

v0:
```python
import jax
import jax.numpy as jnp
from jax import lax
from jax.sharding import PartitionSpec as P

DK = 128
DV = 128
CONV = 4
STRETCH = 64


highest = lax.Precision.HIGHEST


def shifted(value, axis, steps):
    count = lax.axis_size(axis)
    first, last = (max(0, -steps), min(count, count - steps))
    return lax.ppermute(value, axis, [(source, source + steps) for source in range(first, last)])


def product(pattern, left_op, right_op):
    return jnp.einsum(pattern, left_op, right_op, precision=highest)


def causal_conv(source, rim_rows, weight):
    extended = jnp.concatenate([rim_rows, source], axis=0).astype(jnp.float32)
    tap_weights = weight.astype(jnp.float32)
    tok_rows = source.shape[0]
    summed = tap_weights[0] * extended[0:tok_rows]
    for tap_index in range(1, tap_weights.shape[0]):
        summed = summed + tap_weights[tap_index] * extended[tap_index : tap_index + tok_rows]
    return jax.nn.silu(summed)


def stretch_parts(queries, keys_unit, values, log_gates, beta_gates):
    block_len = log_gates.shape[-1]
    cumulative = jnp.cumsum(log_gates, axis=-1)
    row_ids = lax.broadcasted_iota(jnp.int32, (block_len, block_len), 0)
    col_ids = lax.broadcasted_iota(jnp.int32, (block_len, block_len), 1)
    lower_mask = row_ids >= col_ids
    strict_mask = row_ids > col_ids
    gap_log = cumulative[..., :, None] - cumulative[..., None, :]
    decay_mat = jnp.where(lower_mask, jnp.exp(jnp.where(lower_mask, gap_log, 0.0)), 0.0)
    key_grams = product("...cd,...ed->...ce", keys_unit, keys_unit)
    strict_mat = jnp.where(strict_mask, key_grams * decay_mat, 0.0) * beta_gates[..., :, None]
    unit_mat = jnp.eye(block_len, dtype=jnp.float32)
    right_side = beta_gates[..., None] * jnp.concatenate(
        [keys_unit * jnp.exp(cumulative)[..., None], values], axis=-1
    )
    solved = lax.linalg.triangular_solve(
        unit_mat + strict_mat, right_side, left_side=True, lower=True, unit_diagonal=True
    )
    key_width = keys_unit.shape[-1]
    wy_keys = solved[..., :key_width]
    wy_values = solved[..., key_width:]
    q_decayed = queries * jnp.exp(cumulative)[..., None]
    qk_decayed = product("...cd,...ed->...ce", queries, keys_unit) * decay_mat
    k_decayed = keys_unit * jnp.exp(cumulative[..., -1:] - cumulative)[..., None]
    stretch_decay = jnp.exp(cumulative[..., -1])
    return (wy_keys, wy_values, q_decayed, qk_decayed, k_decayed, stretch_decay)


def per_device(
    query_in, key_in, value_in, log_decay, beta_gate, conv_query, conv_key, conv_value, norm_gain
):
    tok_rows = query_in.shape[0]
    query_width = query_in.shape[1]
    key_heads = query_width // DK
    value_heads = value_in.shape[1] // DV
    head_group = value_heads // key_heads
    tails = jnp.concatenate(
        [
            query_in[tok_rows - CONV + 1 :],
            key_in[tok_rows - CONV + 1 :],
            value_in[tok_rows - CONV + 1 :],
        ],
        axis=1,
    )
    before = shifted(tails, ("inner", "outer"), 1)
    query_feat = causal_conv(query_in, before[:, :query_width], conv_query)
    key_feat = causal_conv(key_in, before[:, query_width : 2 * query_width], conv_key)
    value_feat = causal_conv(value_in, before[:, 2 * query_width :], conv_value)
    keys_unit = key_feat.reshape(tok_rows, key_heads, DK)
    keys_unit = keys_unit / jnp.sqrt(jnp.sum(keys_unit * keys_unit, axis=-1, keepdims=True) + 1e-06)
    keys_unit = jnp.repeat(keys_unit, head_group, axis=1)
    queries = jnp.repeat(query_feat.reshape(tok_rows, key_heads, DK), head_group, axis=1)
    values = value_feat.reshape(tok_rows, value_heads, DV)

    def blocked(feature):
        return jnp.transpose(feature, (1, 0, 2)).reshape(
            value_heads, tok_rows // STRETCH, STRETCH, feature.shape[2]
        )

    def gate_blocks(gates):
        return jnp.transpose(gates).reshape(value_heads, tok_rows // STRETCH, STRETCH)

    stretch_terms = stretch_parts(
        blocked(queries),
        blocked(keys_unit),
        blocked(values),
        gate_blocks(log_decay),
        gate_blocks(beta_gate),
    )
    by_stretch = tuple((jnp.moveaxis(term, 1, 0) for term in stretch_terms))
    unit_maps = jnp.broadcast_to(jnp.eye(DK, dtype=jnp.float32), (value_heads, DK, DK))
    empty_state = jnp.zeros((value_heads, DK, DV), jnp.float32)
    start_aug = jnp.concatenate([empty_state, unit_maps], axis=-1)

    def local_step(running, stretch_in):
        wy_keys, wy_values, q_decayed, qk_decayed, k_decayed, stretch_decay = stretch_in
        padded_values = jnp.concatenate(
            [wy_values, jnp.zeros(wy_values.shape[:-1] + (DK,), jnp.float32)], axis=-1
        )
        new_values = padded_values - product("hcd,hde->hce", wy_keys, running)
        advanced = stretch_decay[:, None, None] * running + product(
            "hcd,hce->hde", k_decayed, new_values
        )
        emitted = None
        return (advanced, emitted)

    end_aug, emitted_aug = lax.scan(local_step, start_aug, by_stretch)
    own_add = end_aug[..., :DV]
    own_map = end_aug[..., DV:]
    device_total = lax.axis_size("inner") * lax.axis_size("outer")

    def relay_step(hop_index, carried):
        return shifted(product("hij,hjk->hik", own_map, carried) + own_add, ("inner", "outer"), 1)

    initial = lax.fori_loop(0, device_total - 1, relay_step, empty_state)

    def final_step(running, stretch_in):
        wy_keys, wy_values, q_decayed, qk_decayed, k_decayed, stretch_decay = stretch_in
        new_values = wy_values - product("hcd,hde->hce", wy_keys, running)
        emitted = product("hcd,hde->hce", q_decayed, running) + product(
            "hce,hed->hcd", qk_decayed, new_values
        )
        advanced = stretch_decay[:, None, None] * running + product(
            "hcd,hce->hde", k_decayed, new_values
        )
        return (advanced, emitted)

    final_state, outputs = lax.scan(final_step, initial, by_stretch)
    recurrent = jnp.transpose(outputs, (0, 2, 1, 3)).reshape(tok_rows, value_heads, DV)
    inv_rms = 1.0 / jnp.sqrt(jnp.mean(recurrent * recurrent, axis=-1, keepdims=True) + 1e-06)
    gain_rows = norm_gain.reshape(value_heads, DV)
    return (
        (recurrent * inv_rms * gain_rows).reshape(tok_rows, value_heads * DV).astype(jnp.bfloat16)
    )


def solution(mesh):
    in_specs = (
        P(("inner", "outer"), "head"),
        P(("inner", "outer"), "head"),
        P(("inner", "outer"), "head"),
        P(("inner", "outer"), "head"),
        P(("inner", "outer"), "head"),
        P(None, "head"),
        P(None, "head"),
        P(None, "head"),
        P("head"),
    )
    out_specs = P(("inner", "outer"), "head")
    return jax.shard_map(
        per_device, mesh=mesh, in_specs=in_specs, out_specs=out_specs, check_vma=False
    )
```

profile of v0, /device:TPU:102, one launch (start us, length us, event | category | flops | bytes accessed | tf_op | source)
XLA Modules:
  0.0 944.7 jit_solution(997975998917666296)
XLA Ops:
  13.1 4.0 copy.129
  27.0 4.9 broadcast_divide_fusion
  38.2 8.1 fusion.50
  46.3 7.0 copy.127
  53.3 10.5 %add_bitcast_fusion = f32[4,32,1,64,64]{1,4,3,2,0:T(8,128)} fusion(f32[4,32,64,64]{1,3,2,0:T(8,128)} %copy.127, f32[64,64]{1,0:T(8,128)S(1)} %fusion.42, f32[4,32,64]{1,2,0:T(8,128)S(1)} %copy.128, f32[4,32,64]{1,2,0:T(8,128)S(1)} %copy.125, f32[64,64]{1,0:T(8,128)S(1)} %get-tuple-element.263, pred[64,64]{1,0:T(8,128)(4,1)S(1)} %get-tuple-element.260, ...), kind=kLoop, calls=%fused_computation.36 | loop fusion | flops 4718592 | bytes 4304896 | tf_op jit(solution)/shard_map/triangular_solve | solution.py:50
  63.8 265.0 %custom-call.3 = f32[4,32,1,64,64]{1,3,4,2,0:T(8,128)} custom-call(f32[4,32,1,64,64]{1,4,3,2,0:T(8,128)} %add_bitcast_fusion), custom_call_target="InvertDiagBlocksLowerTriangular" | custom-call | tf_op jit(solution)/shard_map/triangular_solve | solution.py:50
  328.9 9.2 copy.131
  341.0 5.2 divide_multiply_fusion
  346.2 5.3 copy.130
  360.4 10.7 %fusion.23 = f32[4,32,64,256]{3,2,1,0:T(8,128)S(1)} fusion(f32[4,32,64,64]{3,2,1,0:T(8,128)S(1)} %copy-done.3, f32[4,32,64,128]{3,2,1,0:T(8,128)} %bitcast.157, f32[4,32,64,128]{3,2,1,0:T(8,128)S(1)} %get-tuple-element.239, f32[4,32,64]{2,1,0:T(8,128)S(1)} %mul.242), kind=kOutput, calls=%fused_computation.33 | convolution fusion | flops 1614807040 | bytes 18907136 | tf_op jit(solution)/shard_map/triangular_solve | solution.py:50
  373.9 4.8 copy.134
  383.2 147.6 %while.32 = (s32[]{:T(128)}, f32[4,128,256]{2,1,0:T(8,128)S(1)}, f32[32,4]{1,0:T(8,128)}, f32[32,4,64,128]{3,2,1,0:T(8,128)}, f32[32,4,64,128]{3,2,1,0:T(8,128)}, /*index=5*/f32[32,4,64,128]{3,2,1,0:T(8,128)}, s32[]{:T(128)}) while((s32[]{:T(128)}, f32[4,128,256]{2,1,0:T(8,128)S(1)}, f32[32,4]{1,0:T(8,128)}, f32[32,4,64,128]{3,2,1,0:T(8,128)}, ...), condition=%wide.region_3.4_spmd, body=%wide.region_2.3_spmd.sunk | while | flops 201654272 | bytes 2753669 | solution.py:121
  530.8 12.3 %bitcast_multiply_fusion.1 = f32[32,4,64,64]{3,2,0,1:T(8,128)} fusion(f32[4,32,64,128]{3,2,1,0:T(8,128)} %bitcast.152, f32[4,32,64,128]{3,2,1,0:T(8,128)} %bitcast.149, f32[32,4,64]{2,0,1:T(8,128)S(1)} %bitcast.160, pred[64,64]{1,0:T(8,128)(4,1)S(1)} %get-tuple-element.260), kind=kOutput, calls=%fused_computation.49 | convolution fusion | flops 807403520 | bytes 10522624 | tf_op jit(solution)/shard_map/...cd,...ed->...ce/dot_general | solution.py:22
  543.1 171.2 %while.33 = (s32[]{:T(128)}, f32[4,128,128]{2,1,0:T(8,128)S(1)}, f32[4,128,128]{2,1,0:T(8,128)S(1)}, f32[4,128,128]{2,1,0:T(8,128)S(1)}, s32[]{:T(128)}) while((s32[]{:T(128)}, f32[4,128,128]{2,1,0:T(8,128)S(1)}, f32[4,128,128]{2,1,0:T(8,128)S(1)}, f32[4,128,128]{2,1,0:T(8,128)S(1)}, s32[]{:T(128)}) %tuple.76), condition=%wide.region_5.6_spmd, body=%wide.region_4.5_spmd.sunk | while | flops 100728832 | bytes 2097253 | solution.py:129
  547.0 8.3 collective-permute-done
  557.6 8.9 collective-permute-done
  568.9 8.4 collective-permute-done
  579.7 8.4 collective-permute-done
  590.5 8.4 collective-permute-done
  601.2 8.4 collective-permute-done
  612.0 9.4 collective-permute-done
  623.7 10.6 %collective-permute-done = f32[4,128,128]{2,1,0:T(8,128)S(1)} collective-permute-done((f32[4,128,128]{2,1,0:T(8,128)S(1)}, f32[4,128,128]{2,1,0:T(8,128)S(1)}, u32[]{:S(2)}, u32[]{:S(2)}) %collective-permute-start) | collective-permute-done | bytes 262176 | tf_op jit(solution)/shard_map/while/body/eval_jaxpr/ppermute | solution.py:18
  636.7 10.8 %collective-permute-done = f32[4,128,128]{2,1,0:T(8,128)S(1)} collective-permute-done((f32[4,128,128]{2,1,0:T(8,128)S(1)}, f32[4,128,128]{2,1,0:T(8,128)S(1)}, u32[]{:S(2)}, u32[]{:S(2)}) %collective-permute-start) | collective-permute-done | bytes 262176 | tf_op jit(solution)/shard_map/while/body/eval_jaxpr/ppermute | solution.py:18
  649.8 10.0 %collective-permute-done = f32[4,128,128]{2,1,0:T(8,128)S(1)} collective-permute-done((f32[4,128,128]{2,1,0:T(8,128)S(1)}, f32[4,128,128]{2,1,0:T(8,128)S(1)}, u32[]{:S(2)}, u32[]{:S(2)}) %collective-permute-start) | collective-permute-done | bytes 262176 | tf_op jit(solution)/shard_map/while/body/eval_jaxpr/ppermute | solution.py:18
  662.1 9.1 collective-permute-done
  673.5 8.4 collective-permute-done
  684.3 8.4 collective-permute-done
  695.1 8.4 collective-permute-done
  705.8 8.4 collective-permute-done
  714.3 213.5 %while.34 = (s32[]{:T(128)}, f32[4,128,128]{2,1,0:T(8,128)S(1)}, f32[32,4,64,128]{3,2,1,0:T(8,128)}, f32[32,4]{1,0:T(8,128)}, f32[32,4,64,128]{3,2,1,0:T(8,128)}...) while((s32[]{:T(128)}, f32[4,128,128]{2,1,0:T(8,128)S(1)}, ...), condition=%wide.region_7.8_spmd, body=%wide.region_6.7_spmd.sunk | while | flops 176357376 | bytes 2493593 | solution.py:142
  931.6 5.8 copy.144
  937.4 4.7 mul.278
  (406 shorter events, 449.2 us)
Async XLA Ops:
  0.0 18.1 %copy-start.5 = (bf16[2048,256]{1,0:T(8,128)(2,1)S(1)}, bf16[2048,256]{1,0:T(8,128)(2,1)}, u32[]{:S(2)}) copy-start(bf16[2048,256]{1,0:T(8,128)(2,1)} %param.16) | copy-start | bytes 3145732
  0.0 17.1 %copy-start.8 = (f32[2048,4]{0,1:T(4,128)S(1)}, f32[2048,4]{0,1:T(4,128)}, u32[]{:S(2)}) copy-start(f32[2048,4]{0,1:T(4,128)} %param.19) | copy-start | bytes 98308
  2.4 15.6 %collective-permute-start.1 = (bf16[3,1024]{0,1:T(8,128)(2,1)S(1)}, bf16[3,1024]{0,1:T(8,128)(2,1)S(1)}, u32[]{:S(2)}, u32[]{:S(2)}) collective-permute-start(bf16[3,1024]{0,1:T(8,128)(2,1)S(1)} %copy.122), channel_id=1, source_target_pairs={{0,1},{1,2},{2,3},{3,4},{4,5},{5,6},{6,7},{7,8},{8,9},{9,10},{10,1... | collective-permute-start | bytes 18440 | tf_op jit(solution)/shard_map/ppermute | solution.py:18
  46.3 7.0 copy-start.6
  46.3 7.0 copy-start.7
  338.1 2.8 copy-start.9
  338.1 2.9 copy-start.10
  338.1 2.9 copy-start.11
  338.1 2.9 copy-start.12
  346.2 5.4 copy-start.13
  346.2 5.4 copy-start.14
  346.2 5.4 copy-start.15
  346.2 5.4 copy-start.16
  352.9 3.7 copy-start.1
  353.1 7.2 copy-start.2
  356.6 3.8 copy-start.3
  543.5 11.8 %collective-permute-start = (f32[4,128,128]{2,1,0:T(8,128)S(1)}, f32[4,128,128]{2,1,0:T(8,128)S(1)}, u32[]{:S(2)}, u32[]{:S(2)}) collective-permute-start(f32[4,128,128]{2,1,0:T(8,128)S(1)} %convolution_add_fusion.8), channel_id=1, source_target_pairs={{0,1},{1,2},{2,3},{3,4},{4,5},{5,6},{6,7},{7,8},{8,9},{9,10},{10,1... | collective-permute-start | bytes 786440 | tf_op jit(solution)/shard_map/while/body/eval_jaxpr/ppermute | solution.py:18
  555.7 10.9 %collective-permute-start = (f32[4,128,128]{2,1,0:T(8,128)S(1)}, f32[4,128,128]{2,1,0:T(8,128)S(1)}, u32[]{:S(2)}, u32[]{:S(2)}) collective-permute-start(f32[4,128,128]{2,1,0:T(8,128)S(1)} %convolution_add_fusion.8), channel_id=1, source_target_pairs={{0,1},{1,2},{2,3},{3,4},{4,5},{5,6},{6,7},{7,8},{8,9},{9,10},{10,1... | collective-permute-start | bytes 786440 | tf_op jit(solution)/shard_map/while/body/eval_jaxpr/ppermute | solution.py:18
  567.0 10.4 %collective-permute-start = (f32[4,128,128]{2,1,0:T(8,128)S(1)}, f32[4,128,128]{2,1,0:T(8,128)S(1)}, u32[]{:S(2)}, u32[]{:S(2)}) collective-permute-start(f32[4,128,128]{2,1,0:T(8,128)S(1)} %convolution_add_fusion.8), channel_id=1, source_target_pairs={{0,1},{1,2},{2,3},{3,4},{4,5},{5,6},{6,7},{7,8},{8,9},{9,10},{10,1... | collective-permute-start | bytes 786440 | tf_op jit(solution)/shard_map/while/body/eval_jaxpr/ppermute | solution.py:18
  577.8 10.4 %collective-permute-start = (f32[4,128,128]{2,1,0:T(8,128)S(1)}, f32[4,128,128]{2,1,0:T(8,128)S(1)}, u32[]{:S(2)}, u32[]{:S(2)}) collective-permute-start(f32[4,128,128]{2,1,0:T(8,128)S(1)} %convolution_add_fusion.8), channel_id=1, source_target_pairs={{0,1},{1,2},{2,3},{3,4},{4,5},{5,6},{6,7},{7,8},{8,9},{9,10},{10,1... | collective-permute-start | bytes 786440 | tf_op jit(solution)/shard_map/while/body/eval_jaxpr/ppermute | solution.py:18
  588.5 10.4 %collective-permute-start = (f32[4,128,128]{2,1,0:T(8,128)S(1)}, f32[4,128,128]{2,1,0:T(8,128)S(1)}, u32[]{:S(2)}, u32[]{:S(2)}) collective-permute-start(f32[4,128,128]{2,1,0:T(8,128)S(1)} %convolution_add_fusion.8), channel_id=1, source_target_pairs={{0,1},{1,2},{2,3},{3,4},{4,5},{5,6},{6,7},{7,8},{8,9},{9,10},{10,1... | collective-permute-start | bytes 786440 | tf_op jit(solution)/shard_map/while/body/eval_jaxpr/ppermute | solution.py:18
  599.3 10.4 %collective-permute-start = (f32[4,128,128]{2,1,0:T(8,128)S(1)}, f32[4,128,128]{2,1,0:T(8,128)S(1)}, u32[]{:S(2)}, u32[]{:S(2)}) collective-permute-start(f32[4,128,128]{2,1,0:T(8,128)S(1)} %convolution_add_fusion.8), channel_id=1, source_target_pairs={{0,1},{1,2},{2,3},{3,4},{4,5},{5,6},{6,7},{7,8},{8,9},{9,10},{10,1... | collective-permute-start | bytes 786440 | tf_op jit(solution)/shard_map/while/body/eval_jaxpr/ppermute | solution.py:18
  610.1 11.3 %collective-permute-start = (f32[4,128,128]{2,1,0:T(8,128)S(1)}, f32[4,128,128]{2,1,0:T(8,128)S(1)}, u32[]{:S(2)}, u32[]{:S(2)}) collective-permute-start(f32[4,128,128]{2,1,0:T(8,128)S(1)} %convolution_add_fusion.8), channel_id=1, source_target_pairs={{0,1},{1,2},{2,3},{3,4},{4,5},{5,6},{6,7},{7,8},{8,9},{9,10},{10,1... | collective-permute-start | bytes 786440 | tf_op jit(solution)/shard_map/while/body/eval_jaxpr/ppermute | solution.py:18
  621.8 12.5 %collective-permute-start = (f32[4,128,128]{2,1,0:T(8,128)S(1)}, f32[4,128,128]{2,1,0:T(8,128)S(1)}, u32[]{:S(2)}, u32[]{:S(2)}) collective-permute-start(f32[4,128,128]{2,1,0:T(8,128)S(1)} %convolution_add_fusion.8), channel_id=1, source_target_pairs={{0,1},{1,2},{2,3},{3,4},{4,5},{5,6},{6,7},{7,8},{8,9},{9,10},{10,1... | collective-permute-start | bytes 786440 | tf_op jit(solution)/shard_map/while/body/eval_jaxpr/ppermute | solution.py:18
  634.7 12.7 %collective-permute-start = (f32[4,128,128]{2,1,0:T(8,128)S(1)}, f32[4,128,128]{2,1,0:T(8,128)S(1)}, u32[]{:S(2)}, u32[]{:S(2)}) collective-permute-start(f32[4,128,128]{2,1,0:T(8,128)S(1)} %convolution_add_fusion.8), channel_id=1, source_target_pairs={{0,1},{1,2},{2,3},{3,4},{4,5},{5,6},{6,7},{7,8},{8,9},{9,10},{10,1... | collective-permute-start | bytes 786440 | tf_op jit(solution)/shard_map/while/body/eval_jaxpr/ppermute | solution.py:18
  647.8 11.9 %collective-permute-start = (f32[4,128,128]{2,1,0:T(8,128)S(1)}, f32[4,128,128]{2,1,0:T(8,128)S(1)}, u32[]{:S(2)}, u32[]{:S(2)}) collective-permute-start(f32[4,128,128]{2,1,0:T(8,128)S(1)} %convolution_add_fusion.8), channel_id=1, source_target_pairs={{0,1},{1,2},{2,3},{3,4},{4,5},{5,6},{6,7},{7,8},{8,9},{9,10},{10,1... | collective-permute-start | bytes 786440 | tf_op jit(solution)/shard_map/while/body/eval_jaxpr/ppermute | solution.py:18
  660.2 11.0 %collective-permute-start = (f32[4,128,128]{2,1,0:T(8,128)S(1)}, f32[4,128,128]{2,1,0:T(8,128)S(1)}, u32[]{:S(2)}, u32[]{:S(2)}) collective-permute-start(f32[4,128,128]{2,1,0:T(8,128)S(1)} %convolution_add_fusion.8), channel_id=1, source_target_pairs={{0,1},{1,2},{2,3},{3,4},{4,5},{5,6},{6,7},{7,8},{8,9},{9,10},{10,1... | collective-permute-start | bytes 786440 | tf_op jit(solution)/shard_map/while/body/eval_jaxpr/ppermute | solution.py:18
  671.6 10.4 %collective-permute-start = (f32[4,128,128]{2,1,0:T(8,128)S(1)}, f32[4,128,128]{2,1,0:T(8,128)S(1)}, u32[]{:S(2)}, u32[]{:S(2)}) collective-permute-start(f32[4,128,128]{2,1,0:T(8,128)S(1)} %convolution_add_fusion.8), channel_id=1, source_target_pairs={{0,1},{1,2},{2,3},{3,4},{4,5},{5,6},{6,7},{7,8},{8,9},{9,10},{10,1... | collective-permute-start | bytes 786440 | tf_op jit(solution)/shard_map/while/body/eval_jaxpr/ppermute | solution.py:18
  682.4 10.4 %collective-permute-start = (f32[4,128,128]{2,1,0:T(8,128)S(1)}, f32[4,128,128]{2,1,0:T(8,128)S(1)}, u32[]{:S(2)}, u32[]{:S(2)}) collective-permute-start(f32[4,128,128]{2,1,0:T(8,128)S(1)} %convolution_add_fusion.8), channel_id=1, source_target_pairs={{0,1},{1,2},{2,3},{3,4},{4,5},{5,6},{6,7},{7,8},{8,9},{9,10},{10,1... | collective-permute-start | bytes 786440 | tf_op jit(solution)/shard_map/while/body/eval_jaxpr/ppermute | solution.py:18
  693.1 10.4 %collective-permute-start = (f32[4,128,128]{2,1,0:T(8,128)S(1)}, f32[4,128,128]{2,1,0:T(8,128)S(1)}, u32[]{:S(2)}, u32[]{:S(2)}) collective-permute-start(f32[4,128,128]{2,1,0:T(8,128)S(1)} %convolution_add_fusion.8), channel_id=1, source_target_pairs={{0,1},{1,2},{2,3},{3,4},{4,5},{5,6},{6,7},{7,8},{8,9},{9,10},{10,1... | collective-permute-start | bytes 786440 | tf_op jit(solution)/shard_map/while/body/eval_jaxpr/ppermute | solution.py:18
  703.9 10.4 %collective-permute-start = (f32[4,128,128]{2,1,0:T(8,128)S(1)}, f32[4,128,128]{2,1,0:T(8,128)S(1)}, u32[]{:S(2)}, u32[]{:S(2)}) collective-permute-start(f32[4,128,128]{2,1,0:T(8,128)S(1)} %convolution_add_fusion.8), channel_id=1, source_target_pairs={{0,1},{1,2},{2,3},{3,4},{4,5},{5,6},{6,7},{7,8},{8,9},{9,10},{10,1... | collective-permute-start | bytes 786440 | tf_op jit(solution)/shard_map/while/body/eval_jaxpr/ppermute | solution.py:18
  937.3 4.7 copy-start.17
  (2 other events, 3.9 us)
where the time goes:
time: 961 us; the launch traced here: 945 us
  matrix products  322 us (34%)
  other arithmetic  310 us (32%)
  local copies, waits for them, and re-layouts  141 us (15%)
  waiting for transfers between devices  135 us (14%)
  starting transfers between devices  33.9 us (4%)
    dot_general x209, matrix products, product(): return jnp.einsum(pattern, left_op, right_op, precision=highest)  312 us
    another operation x5, other arithmetic, stretch_parts(): lax.linalg.triangular_solve(unit_mat + strict_mat, right_side, left_side=...  276 us
    ppermute x16, waiting for transfers between devices, shifted(): lax.ppermute(value, axis, [(source, source + steps) for source in range(f...  135 us
    ppermute x16, starting transfers between devices, shifted(): lax.ppermute(value, axis, [(source, source + steps) for source in range(f...  33.9 us
    squeeze x32, local copies, waits for them, and re-layouts, per_device(): end_aug, emitted_aug = lax.scan(local_step, start_aug, by_stretch)  29.4 us
    mul x32, local copies, waits for them, and re-layouts, local_step(): stretch_decay[:, None, None] * running  22 us
    mul x32, local copies, waits for them, and re-layouts, final_step(): stretch_decay[:, None, None] * running  21.8 us
  transfers between devices with their start and end apart: 16, of which 15 were waited for; matrix products, arithmetic and copies ran while one was open for 1% of the time, Pallas kernels for 0%

commit v1 on v0

v1 whole, which is shorter than its diff:
```python
import jax
import jax.numpy as jnp
from jax import lax
from jax.experimental import pallas as pl
from jax.experimental.pallas import tpu as pltpu
from jax.sharding import PartitionSpec as P

DK = 128
DV = 128
CONV = 4
SPAN = 256
HALF = 128
BASE = 16
VMEM_BYTES = 56 * 1024 * 1024

f32 = jnp.float32
bf16 = jnp.bfloat16


def shifted(value, axis, steps, wrap):
    count = lax.axis_size(axis)
    if wrap:
        pairs = [(source, (source + steps) % count) for source in range(count)]
    else:
        pairs = [(source, source + steps) for source in range(count - steps)]
    return lax.ppermute(value, axis, pairs)


def split(value):
    high = value.astype(bf16)
    return high, (value - high.astype(f32)).astype(bf16)


def dot(left, right):
    return jnp.dot(left, right, preferred_element_type=f32)


def beside(*parts):
    return jnp.concatenate(parts, axis=1)


def above(*parts):
    return jnp.concatenate(parts, axis=0)


def product(left, right):
    if left[0].shape[1] == HALF:
        return dot(beside(*left), above(right[0], right[0])) + dot(left[0], right[1])
    return dot(left[0], right[0]) + dot(left[1], right[0]) + dot(left[0], right[1])


def product_small(left, right):
    pair = beside(*right)
    both = dot(beside(*left), above(pair, pair))
    return both[:, :HALF] + both[:, HALF:]


def iotas(shape):
    return lax.broadcasted_iota(jnp.int32, shape, 0), lax.broadcasted_iota(jnp.int32, shape, 1)


def conv_silu(halo_ref, prev_ref, cur_ref, taps_ref, first):
    prev = jnp.where(first, halo_ref[...].astype(f32), prev_ref[...].astype(f32))
    cur = cur_ref[...].astype(f32)
    taps = taps_ref[...].astype(f32)
    extended = above(prev[8:], cur)
    rows = cur.shape[0]
    total = taps[CONV - 1 : CONV] * cur
    for tap in range(CONV - 1):
        start = 8 - (CONV - 1) + tap
        total = total + taps[tap : tap + 1] * extended[start : start + rows]
    return total / (1.0 + jnp.exp(-total))


def decay_blocks(cum_col, cum_row, strict):
    row_ids, col_ids = iotas((HALF, HALF))
    keep = (row_ids > col_ids) if strict else (row_ids >= col_ids)
    top = jnp.exp(jnp.where(keep, cum_col[:HALF] - cum_row[:, :HALF], -1e30))
    low = jnp.exp(cum_col[HALF:] - cum_row[:, :HALF])
    end = jnp.exp(jnp.where(keep, cum_col[HALF:] - cum_row[:, HALF:], -1e30))
    return top, low, end


def state_kernel(
    turn_ref, key_ref, key_prev, key_halo, val_ref, val_prev, val_halo, gate_ref, key_taps, val_taps,
    keyt_out, solved_out, start_out, row_out, col_out, end0, end1, end2, end3,
    run_ref, map_ref, add_ref, fin_ref, level_ref, pick_ref, tri_ref,
):
    step = pl.program_id(0)
    heads = run_ref.shape[0]
    key_heads = key_ref.shape[1] // DK
    group = heads // key_heads
    row_ids, col_ids = iotas((HALF, HALF))
    unit = jnp.where(row_ids == col_ids, 1.0, 0.0).astype(f32)
    base_mask = (row_ids // BASE) == (col_ids // BASE)

    @pl.when(step == 0)
    def _():
        zeros = jnp.zeros((HALF, HALF), f32)
        for head in range(heads):
            run_ref[head, 0] = beside(zeros, unit).astype(bf16)
            run_ref[head, 1] = beside(zeros, zeros).astype(bf16)
            map_ref[head] = beside(unit, zeros).astype(bf16)
            add_ref[head] = zeros
        size = BASE
        for level in range(level_ref.shape[0]):
            picked = (
                (row_ids // (2 * size) == col_ids // (2 * size))
                & (row_ids % (2 * size) >= size)
                & (col_ids % (2 * size) < size)
            )
            level_ref[level] = jnp.where(picked, 1.0, 0.0).astype(bf16)
            size *= 2
        for place in range(BASE - 1):
            chosen = jnp.where(row_ids == (col_ids // BASE) * BASE + place, 1.0, 0.0).astype(bf16)
            pick_ref[:, place * HALF : (place + 1) * HALF] = above(chosen, chosen)
        tri_rows, tri_cols = iotas((SPAN, SPAN))
        tri_ref[...] = jnp.where(tri_rows <= tri_cols, 1.0, 0.0).astype(bf16)

    def advance(head):
        maps = map_ref[head]
        high, low = run_ref[head, 0], run_ref[head, 1]
        moved = dot(maps, above(high, high)) + dot(maps[:, :DK], low)
        return beside(moved[:, :DV] + add_ref[head], moved[:, DV:])

    for head in range(heads):
        high, low = split(advance(head))
        run_ref[head, 0] = high
        run_ref[head, 1] = low
        start_out[0, head, 0] = high
        start_out[0, head, 1] = low

    gates = gate_ref[...]
    is_log = lax.broadcasted_iota(jnp.int32, gates.shape, 0) < heads
    logs = jnp.where(is_log, gates, 0.0)
    logs = above(logs, logs)
    high = logs.astype(bf16)
    rest = logs - high.astype(f32)
    mid = rest.astype(bf16)
    low = (rest - mid.astype(f32)).astype(bf16)
    tri = tri_ref[...]
    cum = (dot(high, tri) + dot(mid, tri) + dot(low, tri))[: gates.shape[0]]
    row_out[...] = cum
    packed = above(
        jnp.where(is_log, cum, gates),
        jnp.exp(cum),
        jnp.zeros((HALF - 2 * gates.shape[0], SPAN), f32),
    )
    cols = packed.T
    col_out[...] = cols

    first = step == 0
    key_feat = conv_silu(key_halo, key_prev, key_ref, key_taps, first)
    val_feat = conv_silu(val_halo, val_prev, val_ref, val_taps, first)

    keys, keys_t, grams = [], [], []
    for key_head in range(key_heads):
        feat = key_feat[:, key_head * DK : (key_head + 1) * DK]
        keyed = feat * lax.rsqrt(jnp.sum(feat * feat, axis=1, keepdims=True) + 1e-6)
        turned = keyed.T
        parts = split(turned)
        keyt_out[0, key_head, 0] = parts[0]
        keyt_out[0, key_head, 1] = parts[1]
        keys.append(keyed)
        keys_t.append(turned)
        grams.append(product(split(keyed), parts))

    diag, below = [], []
    for head in range(heads):
        gram = grams[head // group]
        beta_col = cols[:, heads + head : heads + head + 1]
        top, low, end = decay_blocks(cols[:, head : head + 1], cum[head : head + 1], True)
        diag.append(gram[:HALF, :HALF] * top * beta_col[:HALF])
        below.append(split(gram[HALF:, :HALF] * low * beta_col[HALF:]))
        diag.append(gram[HALF:, HALF:] * end * beta_col[HALF:])

    blocks = HALF // BASE
    compact = above(
        *(jnp.sum(jnp.where(base_mask, item, 0.0).reshape(blocks, BASE, HALF), axis=0) for item in diag)
    )
    spread = dot(beside(*split(compact)), pick_ref[...])
    count = len(diag)
    within = lax.broadcasted_iota(jnp.int32, (count, BASE, HALF), 1)
    lanes = lax.broadcasted_iota(jnp.int32, (count, BASE, HALF), 2)
    small = jnp.where(within == lanes % BASE, 1.0, 0.0).astype(f32)
    for place in range(BASE - 1):
        factor = spread[:, place * HALF : (place + 1) * HALF].reshape(count, BASE, HALF)
        small = small - factor * small[:, place : place + 1, :]
    inverses = [
        jnp.where(base_mask, jnp.broadcast_to(small[item][None], (blocks, BASE, HALF)).reshape(HALF, HALF), 0.0)
        for item in range(count)
    ]
    diag_parts = [split(item) for item in diag]
    for level in range(level_ref.shape[0]):
        mask = level_ref[level]
        inv_parts = [split(item) for item in inverses]
        inner = [
            product_small((item[0] * mask, item[1] * mask), inv)
            for item, inv in zip(diag_parts, inv_parts)
        ]
        inverses = [
            whole - product_small(inv, split(part))
            for whole, inv, part in zip(inverses, inv_parts, inner)
        ]
    inv_parts = [split(item) for item in inverses]

    right, tops, lows = [], [], []
    for head in range(heads):
        beta_col = cols[:, heads + head : heads + head + 1]
        exp_col = cols[:, 2 * heads + head : 2 * heads + head + 1]
        right.append(
            beside(keys[head // group] * (beta_col * exp_col), val_feat[:, head * DV : (head + 1) * DV] * beta_col)
        )
    for head in range(heads):
        tops.append(split(product(inv_parts[2 * head], split(right[head][:HALF]))))
    for head in range(heads):
        rest = right[head][HALF:] - product(below[head], tops[head])
        lows.append(split(product(inv_parts[2 * head + 1], split(rest))))
    for head in range(heads):
        solved = (above(tops[head][0], lows[head][0]), above(tops[head][1], lows[head][1]))
        solved_out[0, head, 0] = solved[0]
        solved_out[0, head, 1] = solved[1]
        cum_row = cum[head : head + 1]
        last = cum_row[:, SPAN - 1 : SPAN]
        faded = split(keys_t[head // group] * jnp.exp(last - cum_row))
        gathered = product(faded, solved)
        maps = unit * jnp.exp(last) - gathered[:, :DK]
        map_ref[head] = beside(*split(maps))
        add_ref[head] = gathered[:, DK:]

    @pl.when(step == pl.num_programs(0) - 1)
    def _():
        for head in range(heads):
            fin_ref[head] = advance(head)
        turn = turn_ref[0]
        for place, end_ref in enumerate((end0, end1, end2, end3)):
            end_ref[...] = fin_ref[lax.rem(turn + place, heads)]


def query_kernel(
    query_ref, query_prev, query_halo, taps_ref, keyt_ref, solved_ref, start_ref, row_ref, col_ref, *rest
):
    local_out, carry_out = rest[-3:-1]
    offset = rest[-1]
    first = pl.program_id(0) + offset == 0
    feat = conv_silu(query_halo, query_prev, query_ref, taps_ref, first)
    key_heads = query_ref.shape[1] // DK
    heads = solved_ref.shape[1]
    group = heads // key_heads
    queries, grams = [], []
    for key_head in range(key_heads):
        query = feat[:, key_head * DK : (key_head + 1) * DK]
        queries.append(query)
        grams.append(product(split(query), (keyt_ref[0, key_head, 0], keyt_ref[0, key_head, 1])))
    lifted = []
    for head in range(heads):
        gram = grams[head // group]
        top, low, end = decay_blocks(col_ref[:, head : head + 1], row_ref[head : head + 1], False)
        high, fine = solved_ref[0, head, 0], solved_ref[0, head, 1]
        upper = product(split(gram[:HALF, :HALF] * top), (high[:HALF], fine[:HALF]))
        wide = beside(gram[HALF:, :HALF] * low, gram[HALF:, HALF:] * end)
        lifted.append(above(upper, product(split(wide), (high, fine))))
    for head in range(heads):
        exp_col = col_ref[:, 2 * heads + head : 2 * heads + head + 1]
        reach = queries[head // group] * exp_col - lifted[head][:, :DK]
        seen = product(split(reach), (start_ref[0, head, 0], start_ref[0, head, 1]))
        local_out[:, head * DV : (head + 1) * DV] = seen[:, :DV] + lifted[head][:, DK:]
        carry_out[:, head * 2 * DK : (head + 1) * 2 * DK] = beside(*split(seen[:, DV:]))


def compose_kernel(turn_ref, part0, part1, part2, part3, total_out, tail_out, prefix_out, all_ref):
    count = all_ref.shape[0]
    turn = turn_ref[0]
    for place, part in enumerate((part0, part1, part2, part3)):
        all_ref[lax.rem(turn + count - place, count)] = part[...]
    running = all_ref[0]
    prefix_out[0] = running
    for member in range(1, count):
        own = all_ref[member]
        moved = product(split(own[:, DV:]), split(running))
        running = beside(moved[:, :DV] + own[:, :DV], moved[:, DV:])
        if member < count - 1:
            prefix_out[member] = running
    total_out[...] = running
    tail_out[...] = running[:, :DV]


def enter_kernel(turn_ref, near_ref, next_ref, far_ref, prefix_ref, out0, out1, out2, out3, all_ref):
    count = all_ref.shape[0]
    turn = turn_ref[0]
    far = next_ref[:, :DV] + product_small(split(next_ref[:, DV:]), split(far_ref[...]))
    entry = near_ref[:, :DV] + product_small(split(near_ref[:, DV:]), split(far))
    parts = split(entry)
    all_ref[0] = entry
    for member in range(1, count):
        prefix = prefix_ref[member - 1]
        all_ref[member] = prefix[:, :DV] + product_small(split(prefix[:, DV:]), parts)
    for place, out in enumerate((out0, out1, out2, out3)):
        out[...] = all_ref[lax.rem(turn + place, count)]


def close_kernel(turn_ref, part0, part1, part2, part3, local_ref, carry_ref, gain_ref, out_ref, state_ref):
    heads = state_ref.shape[0]
    turn = turn_ref[0]

    @pl.when(pl.program_id(0) == 0)
    def _():
        for place, part in enumerate((part0, part1, part2, part3)):
            pair = beside(*split(part[...]))
            state_ref[lax.rem(turn + heads - place, heads)] = above(pair, pair)

    for head in range(heads):
        both = dot(carry_ref[:, head * 2 * DK : (head + 1) * 2 * DK], state_ref[head])
        value = local_ref[:, head * DV : (head + 1) * DV] + both[:, :DV] + both[:, DV:]
        scale = lax.rsqrt(jnp.sum(value * value, axis=1, keepdims=True) * (1.0 / DV) + 1e-6)
        gain = gain_ref[:, head * DV : (head + 1) * DV]
        out_ref[:, head * DV : (head + 1) * DV] = (value * scale * gain).astype(bf16)


def whole(shape):
    return pl.BlockSpec(shape, lambda *_: (0,) * len(shape))


def params():
    return pltpu.CompilerParams(dimension_semantics=("arbitrary",), vmem_limit_bytes=VMEM_BYTES)


def cost(flops, size, exps=0):
    return pl.CostEstimate(flops=flops, bytes_accessed=size, transcendentals=exps)


def per_device(
    query_in, key_in, value_in, log_decay, beta_gate, conv_query, conv_key, conv_value, norm_gain
):
    tok_rows, query_width = query_in.shape
    value_width = value_in.shape[1]
    key_heads = query_width // DK
    heads = value_width // DV
    spans = tok_rows // SPAN
    turn = lax.axis_index("outer").astype(jnp.int32).reshape(1)
    tails = beside(query_in[tok_rows - 16 :], key_in[tok_rows - 16 :], value_in[tok_rows - 16 :])
    before = shifted(tails, ("inner", "outer"), 1, False)
    query_halo = before[:, :query_width]
    key_halo = before[:, query_width : 2 * query_width]
    value_halo = before[:, 2 * query_width :]
    gates = above(log_decay.T, beta_gate.T)

    def prev_rows(offset):
        return lambda i, *_: (jnp.maximum((i + offset) * (SPAN // 16) - 1, 0), 0)

    square = jax.ShapeDtypeStruct((DK, 2 * DV), f32)
    keyt, solved, starts, rows, cols, *ends = pl.pallas_call(
        state_kernel,
        grid_spec=pltpu.PrefetchScalarGridSpec(
            num_scalar_prefetch=1,
            grid=(spans,),
            in_specs=[
                pl.BlockSpec((SPAN, query_width), lambda i, *_: (i, 0)),
                pl.BlockSpec((16, query_width), prev_rows(0)),
                whole((16, query_width)),
                pl.BlockSpec((SPAN, value_width), lambda i, *_: (i, 0)),
                pl.BlockSpec((16, value_width), prev_rows(0)),
                whole((16, value_width)),
                pl.BlockSpec((2 * heads, SPAN), lambda i, *_: (0, i)),
                whole((CONV, query_width)),
                whole((CONV, value_width)),
            ],
            out_specs=[
                pl.BlockSpec((1, key_heads, 2, DK, SPAN), lambda i, *_: (i, 0, 0, 0, 0)),
                pl.BlockSpec((1, heads, 2, SPAN, 2 * DV), lambda i, *_: (i, 0, 0, 0, 0)),
                pl.BlockSpec((1, heads, 2, DK, 2 * DV), lambda i, *_: (i, 0, 0, 0, 0)),
                pl.BlockSpec((2 * heads, SPAN), lambda i, *_: (0, i)),
                pl.BlockSpec((SPAN, HALF), lambda i, *_: (i, 0)),
            ]
            + [whole((DK, 2 * DV))] * 4,
            scratch_shapes=[
                pltpu.VMEM((heads, 2, DK, 2 * DV), bf16),
                pltpu.VMEM((heads, DK, 2 * DK), bf16),
                pltpu.VMEM((heads, DK, DV), f32),
                pltpu.VMEM((heads, DK, 2 * DV), f32),
                pltpu.VMEM((3, HALF, HALF), bf16),
                pltpu.VMEM((2 * HALF, (BASE - 1) * HALF), bf16),
                pltpu.VMEM((SPAN, SPAN), bf16),
            ],
        ),
        out_shape=[
            jax.ShapeDtypeStruct((spans, key_heads, 2, DK, SPAN), bf16),
            jax.ShapeDtypeStruct((spans, heads, 2, SPAN, 2 * DV), bf16),
            jax.ShapeDtypeStruct((spans, heads, 2, DK, 2 * DV), bf16),
            jax.ShapeDtypeStruct((2 * heads, tok_rows), f32),
            jax.ShapeDtypeStruct((tok_rows, HALF), f32),
        ]
        + [square] * 4,
        compiler_params=params(),
        cost_estimate=cost(20_000_000_000, 20_000_000),
        name="state_path",
    )(turn, key_in, key_in, key_halo, value_in, value_in, value_halo, gates, conv_key, conv_value)

    parts = [ends[0]] + [shifted(ends[k], "outer", k, True) for k in (1, 2, 3)]

    out_types = (
        jax.ShapeDtypeStruct((tok_rows, value_width), f32),
        jax.ShapeDtypeStruct((tok_rows, 2 * value_width), bf16),
    )

    def query_part(offset, count, earlier):
        def body(*refs):
            query_kernel(*refs, offset)

        def at(i):
            return i + offset

        return pl.pallas_call(
            body,
            grid=(count,),
            in_specs=[
                pl.BlockSpec((SPAN, query_width), lambda i: (at(i), 0)),
                pl.BlockSpec((16, query_width), prev_rows(offset)),
                whole((16, query_width)),
                whole((CONV, query_width)),
                pl.BlockSpec((1, key_heads, 2, DK, SPAN), lambda i: (at(i), 0, 0, 0, 0)),
                pl.BlockSpec((1, heads, 2, SPAN, 2 * DV), lambda i: (at(i), 0, 0, 0, 0)),
                pl.BlockSpec((1, heads, 2, DK, 2 * DV), lambda i: (at(i), 0, 0, 0, 0)),
                pl.BlockSpec((2 * heads, SPAN), lambda i: (0, at(i))),
                pl.BlockSpec((SPAN, HALF), lambda i: (at(i), 0)),
            ]
            + [pl.BlockSpec(memory_space=pl.ANY)] * len(earlier),
            out_specs=[
                pl.BlockSpec((SPAN, value_width), lambda i: (at(i), 0)),
                pl.BlockSpec((SPAN, 2 * value_width), lambda i: (at(i), 0)),
            ],
            out_shape=out_types,
            input_output_aliases={9 + k: k for k in range(len(earlier))},
            compiler_params=params(),
            cost_estimate=cost(2_000_000_000 * count, 3_000_000 * count),
            name="query_path",
        )(query_in, query_in, query_halo, conv_query, keyt, solved, starts, rows, cols, *earlier)

    first_half = query_part(0, spans // 2, ())

    total, tail, prefix = pl.pallas_call(
        compose_kernel,
        grid_spec=pltpu.PrefetchScalarGridSpec(
            num_scalar_prefetch=1,
            grid=(1,),
            in_specs=[whole((DK, 2 * DV))] * 4,
            out_specs=[whole((DK, 2 * DV)), whole((DK, DV)), whole((3, DK, 2 * DV))],
            scratch_shapes=[pltpu.VMEM((4, DK, 2 * DV), f32)],
        ),
        out_shape=[
            square,
            jax.ShapeDtypeStruct((DK, DV), f32),
            jax.ShapeDtypeStruct((3, DK, 2 * DV), f32),
        ],
        compiler_params=params(),
        cost_estimate=cost(100_000_000, 1_000_000),
        name="compose",
    )(turn, *parts)
    near = shifted(total, "inner", 1, False)
    middle = shifted(total, "inner", 2, False)
    far = shifted(tail, "inner", 3, False)

    local, carry = query_part(spans // 2, spans - spans // 2, first_half)

    entries = pl.pallas_call(
        enter_kernel,
        grid_spec=pltpu.PrefetchScalarGridSpec(
            num_scalar_prefetch=1,
            grid=(1,),
            in_specs=[whole((DK, 2 * DV)), whole((DK, 2 * DV)), whole((DK, DV)), whole((3, DK, 2 * DV))],
            out_specs=[whole((DK, DV))] * 4,
            scratch_shapes=[pltpu.VMEM((4, DK, DV), f32)],
        ),
        out_shape=[jax.ShapeDtypeStruct((DK, DV), f32)] * 4,
        compiler_params=params(),
        cost_estimate=cost(50_000_000, 1_000_000),
        name="enter",
    )(turn, near, middle, far, prefix)
    states = [entries[0]] + [shifted(entries[k], "outer", k, True) for k in (1, 2, 3)]

    return pl.pallas_call(
        close_kernel,
        grid_spec=pltpu.PrefetchScalarGridSpec(
            num_scalar_prefetch=1,
            grid=(spans,),
            in_specs=[whole((DK, DV))] * 4
            + [
                pl.BlockSpec((SPAN, value_width), lambda i, *_: (i, 0)),
                pl.BlockSpec((SPAN, 2 * value_width), lambda i, *_: (i, 0)),
                whole((1, value_width)),
            ],
            out_specs=pl.BlockSpec((SPAN, value_width), lambda i, *_: (i, 0)),
            scratch_shapes=[pltpu.VMEM((heads, 2 * DK, 2 * DV), bf16)],
        ),
        out_shape=jax.ShapeDtypeStruct((tok_rows, value_width), bf16),
        compiler_params=params(),
        cost_estimate=cost(2_000_000_000, 10_000_000),
        name="close",
    )(turn, *states, local, carry, norm_gain.reshape(1, value_width))


def solution(mesh):
    in_specs = (
        P(("inner", "outer"), "head"),
        P(("inner", "outer"), "head"),
        P(("inner", "outer"), "head"),
        P(("inner", "outer"), "head"),
        P(("inner", "outer"), "head"),
        P(None, "head"),
        P(None, "head"),
        P(None, "head"),
        P("head"),
    )
    out_specs = P(("inner", "outer"), "head")
    return jax.shard_map(
        per_device, mesh=mesh, in_specs=in_specs, out_specs=out_specs, check_vma=False
    )
```

time: 961 us -> 98.6 us (0.10)
  the two profiles are of different devices: /device:TPU:102 before, /device:TPU:0 now
where the time goes in v1:
time: 98.6 us; the launch traced here: 97.5 us
  Pallas kernels  62.3 us (63%)
  starting transfers between devices  24.3 us (25%)
  local copies, waits for them, and re-layouts  5.32 us (5%)
  waiting for transfers between devices  4 us (4%)
  other arithmetic  1.43 us (1%)
    pallas_call x1, Pallas kernels, per_device(): pl.pallas_call(state_kernel, grid_spec=pltpu.PrefetchScalarGridSpec(num_s...  32.6 us
    ppermute x10, starting transfers between devices, shifted(): return lax.ppermute(value, axis, pairs)  24.3 us
    pallas_call x2, Pallas kernels, query_part(): pl.pallas_call(body, grid=(count,), in_specs=[pl.BlockSpec((SPAN, query_w...  16.4 us
    pallas_call x1, Pallas kernels, per_device(): pl.pallas_call(close_kernel, grid_spec=pltpu.PrefetchScalarGridSpec(num_s...  8.33 us
    ppermute x10, waiting for transfers between devices, shifted(): return lax.ppermute(value, axis, pairs)  4 us
    pallas_call x1, Pallas kernels, per_device(): pl.pallas_call(compose_kernel, grid_spec=pltpu.PrefetchScalarGridSpec(num...  2.57 us
    pallas_call x1, Pallas kernels, per_device(): pl.pallas_call(enter_kernel, grid_spec=pltpu.PrefetchScalarGridSpec(num_s...  2.46 us
    unnamed x18, local copies, waits for them, and re-layouts  2 us
  transfers between devices with their start and end apart: 10, of which 4 were waited for; matrix products, arithmetic and copies ran while one was open for 1% of the time, Pallas kernels for 17%

profile of v1, /device:TPU:0, one launch (start us, length us, event | category | flops | bytes accessed | tf_op | source)
XLA Modules:
  0.0 97.5 jit_solution(13642648330810533888)
XLA Ops:
  0.0 0.7 slice.19
  0.7 0.7 slice.18
  1.4 0.7 slice.20
  2.1 3.6 %collective-permute-start = (bf16[16,1024]{1,0:T(8,128)(2,1)S(1)}, bf16[16,1024]{1,0:T(8,128)(2,1)S(1)}, u32[]{:S(2)}, u32[]{:S(2)}) collective-permute-start(bf16[16,1024]{1,0:T(8,128)(2,1)S(1)} %pad_maximum_fusion.1), channel_id=1, source_target_pairs={{0,1},{1,2},{2,3},{3,4},{4,5},{5,6},{6,7},{7,8},{8,9},{9,10},{10,1... | collective-permute-start | bytes 98312 | tf_op jit(solution)/shard_map/ppermute | solution.py:26
  5.7 1.4 %pad_maximum_fusion.gate_ref = f32[8,2048]{1,0:T(8,128)} fusion(f32[4,2048]{1,0:T(4,128)} %bitcast.4, f32[4,2048]{1,0:T(4,128)} %bitcast.5), kind=kLoop, calls=%fused_computation | loop fusion | flops 16384 | bytes 131072 | tf_op jit(solution)/shard_map/concatenate | solution.py:43
  7.1 0.2 collective-permute-done
  7.3 0.6 slice.25.val_halo
  7.9 0.6 fusion
  8.5 32.6 %state_path.1 = (bf16[8,2,2,128,256]{4,3,2,1,0:T(8,128)(2,1)}, bf16[8,4,2,256,256]{4,3,2,1,0:T(8,128)(2,1)}, bf16[8,4,2,128,256]{4,3,2,1,0:T(8,128)(2,1)}, f32[8...) custom-call(s32[1]{0:T(128)} %bitcast.turn_ref, ...), custom_call_target="tpu_custom_call" | custom-call | flops 20000000000 | bytes 20000000 | tf_op jit(solution)/shard_map/state_path/pallas_call | solution.py:352
  41.1 2.4 %collective-permute-start.1 = (f32[128,256]{1,0:T(8,128)}, f32[128,256]{1,0:T(8,128)S(1)}, u32[]{:S(2)}, u32[]{:S(2)}) collective-permute-start(f32[128,256]{1,0:T(8,128)} %get-tuple-element.26), channel_id=1, source_target_pairs={{0,1},{1,2},{2,3},{3,0},{4,5},{5,6},{6,7},{7,4},{8,9},{9,10},{10,1... | collective-permute-start | bytes 393224 | tf_op jit(solution)/shard_map/ppermute | solution.py:26
  43.4 2.9 %collective-permute-start.2 = (f32[128,256]{1,0:T(8,128)}, f32[128,256]{1,0:T(8,128)S(1)}, u32[]{:S(2)}, u32[]{:S(2)}) collective-permute-start(f32[128,256]{1,0:T(8,128)} %get-tuple-element.27), channel_id=1, source_target_pairs={{0,2},{1,3},{2,0},{3,1},{4,6},{5,7},{6,4},{7,5},{8,10},{9,11},{10,... | collective-permute-start | bytes 393224 | tf_op jit(solution)/shard_map/ppermute | solution.py:26
  46.4 1.3 %collective-permute-start.3 = (f32[128,256]{1,0:T(8,128)}, f32[128,256]{1,0:T(8,128)S(1)}, u32[]{:S(2)}, u32[]{:S(2)}) collective-permute-start(f32[128,256]{1,0:T(8,128)} %get-tuple-element.28), channel_id=1, source_target_pairs={{0,3},{1,0},{2,1},{3,2},{4,7},{5,4},{6,5},{7,6},{8,11},{9,8},{10,9... | collective-permute-start | bytes 393224 | tf_op jit(solution)/shard_map/ppermute | solution.py:26
  47.7 1.8 %collective-permute-done.1.part1 = f32[128,256]{1,0:T(8,128)S(1)} collective-permute-done((f32[128,256]{1,0:T(8,128)}, f32[128,256]{1,0:T(8,128)S(1)}, u32[]{:S(2)}, u32[]{:S(2)}) %collective-permute-start.1) | collective-permute-done | bytes 131104 | tf_op jit(solution)/shard_map/ppermute | solution.py:26
  49.5 2.0 %collective-permute-done.2.part2 = f32[128,256]{1,0:T(8,128)S(1)} collective-permute-done((f32[128,256]{1,0:T(8,128)}, f32[128,256]{1,0:T(8,128)S(1)}, u32[]{:S(2)}, u32[]{:S(2)}) %collective-permute-start.2) | collective-permute-done | bytes 131104 | tf_op jit(solution)/shard_map/ppermute | solution.py:26
  51.5 0.1 collective-permute-done.3.part3
  51.5 0.6 copy-done.3
  52.1 0.1 copy-done.4
  52.2 2.6 %compose.1 = (f32[128,256]{1,0:T(8,128)}, f32[128,128]{1,0:T(8,128)}, f32[3,128,256]{2,1,0:T(8,128)}) custom-call(s32[1]{0:T(128)} %bitcast.turn_ref, f32[128,256]{1,0:T(8,128)} %get-tuple-element.25.part0, f32[128,256]{1,0:T(8,128)} %copy-done.2, f32[128,256]{1,0:T(8,128)} %copy-done.3, f32[128,256]{1,0:T(8,128)} %copy-done.4), custom_call_target="tpu_custom_call" | custom-call | flops 100000000 | bytes 1000000 | tf_op jit(solution)/shard_map/compose/pallas_call | solution.py:441
  54.7 6.4 %collective-permute-start.5 = (f32[128,256]{1,0:T(8,128)}, f32[128,256]{1,0:T(8,128)S(1)}, u32[]{:S(2)}, u32[]{:S(2)}) collective-permute-start(f32[128,256]{1,0:T(8,128)} %get-tuple-element.29), channel_id=1, source_target_pairs={{0,8},{4,12},{1,9},{5,13},{2,10},{6,14},{3,11},{7,15},{16,24},{20,... | collective-permute-start | bytes 393224 | tf_op jit(solution)/shard_map/ppermute | solution.py:26
  61.1 2.5 %collective-permute-start.4 = (f32[128,256]{1,0:T(8,128)}, f32[128,256]{1,0:T(8,128)S(1)}, u32[]{:S(2)}, u32[]{:S(2)}) collective-permute-start(f32[128,256]{1,0:T(8,128)} %get-tuple-element.29), channel_id=1, source_target_pairs={{0,4},{4,8},{8,12},{1,5},{5,9},{9,13},{2,6},{6,10},{10,14},{3,7},{... | collective-permute-start | bytes 393224 | tf_op jit(solution)/shard_map/ppermute | solution.py:26
  63.6 1.3 %collective-permute-start.6 = (f32[128,128]{1,0:T(8,128)}, f32[128,128]{1,0:T(8,128)S(1)}, u32[]{:S(2)}, u32[]{:S(2)}) collective-permute-start(f32[128,128]{1,0:T(8,128)} %get-tuple-element.30), channel_id=1, source_target_pairs={{0,12},{1,13},{2,14},{3,15},{16,28},{17,29},{18,30},{19,31},{32,44... | collective-permute-start | bytes 196616 | tf_op jit(solution)/shard_map/ppermute | solution.py:26
  64.9 8.2 %query_path.2 = (f32[2048,512]{1,0:T(8,128)}, bf16[2048,1024]{1,0:T(8,128)(2,1)}) custom-call(bf16[2048,256]{1,0:T(8,128)(2,1)} %refs_1_.3, bf16[2048,256]{1,0:T(8,128)(2,1)} %refs_1_.3, bf16[16,256]{1,0:T(8,128)(2,1)} %get-tuple-element.45.refs_2_, bf16[4,256]{1,0:T(4,128)(2,1)} %refs_3_.3, bf16[8,2,2,128,256]{4,3,2,1,0:T(8,128)(2,1)} %get-tuple-element.36.refs_4_, ...), custom_call_target="tpu_custom_call" | custom-call | flops 8000000000 | bytes 12000000 | tf_op jit(solution)/shard_map/query_path/pallas_call | solution.py:413
  73.2 0.6 copy-done.8
  73.8 0.1 copy-done
  73.8 0.1 copy-done.1
  73.9 2.5 %enter.1 = (f32[128,128]{1,0:T(8,128)}, f32[128,128]{1,0:T(8,128)}, f32[128,128]{1,0:T(8,128)}, f32[128,128]{1,0:T(8,128)}) custom-call(s32[1]{0:T(128)} %bitcast.turn_ref, f32[128,256]{1,0:T(8,128)} %copy-done.1, f32[128,256]{1,0:T(8,128)} %copy-done, f32[128,128]{1,0:T(8,128)} %copy-done.8, f32[3,128,256]{2,1,0:T(8,128)} %get-tuple-element.31.prefix_ref), custom_call_target="tpu_custom_call" | custom-call | flops 50000000 | bytes 1000000 | tf_op jit(solution)/shard_map/enter/pallas_call | solution.py:465
  76.4 0.4 collective-permute-start.7
  76.8 3.6 %collective-permute-start.8 = (f32[128,128]{1,0:T(8,128)}, f32[128,128]{1,0:T(8,128)S(1)}, u32[]{:S(2)}, u32[]{:S(2)}) collective-permute-start(f32[128,128]{1,0:T(8,128)} %get-tuple-element.34), channel_id=1, source_target_pairs={{0,2},{1,3},{2,0},{3,1},{4,6},{5,7},{6,4},{7,5},{8,10},{9,11},{10,... | collective-permute-start | bytes 196616 | tf_op jit(solution)/shard_map/ppermute | solution.py:26
  80.3 8.2 %query_path.3 = (f32[2048,512]{1,0:T(8,128)}, bf16[2048,1024]{1,0:T(8,128)(2,1)}) custom-call(bf16[2048,256]{1,0:T(8,128)(2,1)} %refs_1_.3, bf16[2048,256]{1,0:T(8,128)(2,1)} %refs_1_.3, bf16[16,256]{1,0:T(8,128)(2,1)} %get-tuple-element.45.refs_2_, bf16[4,256]{1,0:T(4,128)(2,1)} %refs_3_.3, ...), custom_call_target="tpu_custom_call", output_to_operand_aliasing={{0}: (9, {}), {1}: (10, {})} | custom-call | flops 8000000000 | bytes 12000000 | tf_op jit(solution)/shard_map/query_path/pallas_call | solution.py:413
  88.5 0.6 copy-done.5
  89.1 0.0 copy-done.6
  89.2 8.3 %close.1 = bf16[2048,512]{1,0:T(8,128)(2,1)} custom-call(s32[1]{0:T(128)} %bitcast.turn_ref, f32[128,128]{1,0:T(8,128)} %get-tuple-element.32.part0, f32[128,128]{1,0:T(8,128)} %copy-done.5, f32[128,128]{1,0:T(8,128)} %copy-done.6, f32[128,128]{1,0:T(8,128)} %copy-done.7, f32[2048,512]{1,0:T(8,128)} %get-tuple-element.43.local_ref, ...), custom_call_target="tpu_custom_call" | custom-call | flops 2000000000 | bytes 10000000 | tf_op jit(solution)/shard_map/close/pallas_call | solution.py:481
  (19 shorter events, 0.1 us)
Async XLA Ops:
  2.1 5.1 %collective-permute-start = (bf16[16,1024]{1,0:T(8,128)(2,1)S(1)}, bf16[16,1024]{1,0:T(8,128)(2,1)S(1)}, u32[]{:S(2)}, u32[]{:S(2)}) collective-permute-start(bf16[16,1024]{1,0:T(8,128)(2,1)S(1)} %pad_maximum_fusion.1), channel_id=1, source_target_pairs={{0,1},{1,2},{2,3},{3,4},{4,5},{5,6},{6,7},{7,8},{8,9},{9,10},{10,1... | collective-permute-start | bytes 98312 | tf_op jit(solution)/shard_map/ppermute | solution.py:26
  41.1 8.4 %collective-permute-start.1 = (f32[128,256]{1,0:T(8,128)}, f32[128,256]{1,0:T(8,128)S(1)}, u32[]{:S(2)}, u32[]{:S(2)}) collective-permute-start(f32[128,256]{1,0:T(8,128)} %get-tuple-element.26), channel_id=1, source_target_pairs={{0,1},{1,2},{2,3},{3,0},{4,5},{5,6},{6,7},{7,4},{8,9},{9,10},{10,1... | collective-permute-start | bytes 393224 | tf_op jit(solution)/shard_map/ppermute | solution.py:26
  43.4 8.0 %collective-permute-start.2 = (f32[128,256]{1,0:T(8,128)}, f32[128,256]{1,0:T(8,128)S(1)}, u32[]{:S(2)}, u32[]{:S(2)}) collective-permute-start(f32[128,256]{1,0:T(8,128)} %get-tuple-element.27), channel_id=1, source_target_pairs={{0,2},{1,3},{2,0},{3,1},{4,6},{5,7},{6,4},{7,5},{8,10},{9,11},{10,... | collective-permute-start | bytes 393224 | tf_op jit(solution)/shard_map/ppermute | solution.py:26
  46.4 5.2 %collective-permute-start.3 = (f32[128,256]{1,0:T(8,128)}, f32[128,256]{1,0:T(8,128)S(1)}, u32[]{:S(2)}, u32[]{:S(2)}) collective-permute-start(f32[128,256]{1,0:T(8,128)} %get-tuple-element.28), channel_id=1, source_target_pairs={{0,3},{1,0},{2,1},{3,2},{4,7},{5,4},{6,5},{7,6},{8,11},{9,8},{10,9... | collective-permute-start | bytes 393224 | tf_op jit(solution)/shard_map/ppermute | solution.py:26
  49.4 2.1 %copy-start.2 = (f32[128,256]{1,0:T(8,128)}, f32[128,256]{1,0:T(8,128)S(1)}, u32[]{:S(2)}) copy-start(f32[128,256]{1,0:T(8,128)S(1)} %collective-permute-done.1.part1) | copy-start | bytes 393220
  51.5 0.7 copy-start.3
  51.5 0.7 copy-start.4
  54.7 18.4 %collective-permute-start.5 = (f32[128,256]{1,0:T(8,128)}, f32[128,256]{1,0:T(8,128)S(1)}, u32[]{:S(2)}, u32[]{:S(2)}) collective-permute-start(f32[128,256]{1,0:T(8,128)} %get-tuple-element.29), channel_id=1, source_target_pairs={{0,8},{4,12},{1,9},{5,13},{2,10},{6,14},{3,11},{7,15},{16,24},{20,... | collective-permute-start | bytes 393224 | tf_op jit(solution)/shard_map/ppermute | solution.py:26
  61.1 12.1 %collective-permute-start.4 = (f32[128,256]{1,0:T(8,128)}, f32[128,256]{1,0:T(8,128)S(1)}, u32[]{:S(2)}, u32[]{:S(2)}) collective-permute-start(f32[128,256]{1,0:T(8,128)} %get-tuple-element.29), channel_id=1, source_target_pairs={{0,4},{4,8},{8,12},{1,5},{5,9},{9,13},{2,6},{6,10},{10,14},{3,7},{... | collective-permute-start | bytes 393224 | tf_op jit(solution)/shard_map/ppermute | solution.py:26
  63.6 9.5 %collective-permute-start.6 = (f32[128,128]{1,0:T(8,128)}, f32[128,128]{1,0:T(8,128)S(1)}, u32[]{:S(2)}, u32[]{:S(2)}) collective-permute-start(f32[128,128]{1,0:T(8,128)} %get-tuple-element.30), channel_id=1, source_target_pairs={{0,12},{1,13},{2,14},{3,15},{16,28},{17,29},{18,30},{19,31},{32,44... | collective-permute-start | bytes 196616 | tf_op jit(solution)/shard_map/ppermute | solution.py:26
  73.2 0.6 copy-start.8
  73.2 0.7 copy-start
  73.2 0.7 copy-start.1
  76.4 12.1 %collective-permute-start.7 = (f32[128,128]{1,0:T(8,128)}, f32[128,128]{1,0:T(8,128)S(1)}, u32[]{:S(2)}, u32[]{:S(2)}) collective-permute-start(f32[128,128]{1,0:T(8,128)} %get-tuple-element.33), channel_id=1, source_target_pairs={{0,1},{1,2},{2,3},{3,0},{4,5},{5,6},{6,7},{7,4},{8,9},{9,10},{10,1... | collective-permute-start | bytes 196616 | tf_op jit(solution)/shard_map/ppermute | solution.py:26
  76.8 11.8 %collective-permute-start.8 = (f32[128,128]{1,0:T(8,128)}, f32[128,128]{1,0:T(8,128)S(1)}, u32[]{:S(2)}, u32[]{:S(2)}) collective-permute-start(f32[128,128]{1,0:T(8,128)} %get-tuple-element.34), channel_id=1, source_target_pairs={{0,2},{1,3},{2,0},{3,1},{4,6},{5,7},{6,4},{7,5},{8,10},{9,11},{10,... | collective-permute-start | bytes 196616 | tf_op jit(solution)/shard_map/ppermute | solution.py:26
  80.3 8.2 %collective-permute-start.9 = (f32[128,128]{1,0:T(8,128)}, f32[128,128]{1,0:T(8,128)S(1)}, u32[]{:S(2)}, u32[]{:S(2)}) collective-permute-start(f32[128,128]{1,0:T(8,128)} %get-tuple-element.35), channel_id=1, source_target_pairs={{0,3},{1,0},{2,1},{3,2},{4,7},{5,4},{6,5},{7,6},{8,11},{9,8},{10,9... | collective-permute-start | bytes 196616 | tf_op jit(solution)/shard_map/ppermute | solution.py:26
  88.5 0.6 copy-start.5
  88.5 0.6 copy-start.6
  88.5 0.6 copy-start.7

commit v2 on v1

--- a/solution.py
+++ b/solution.py
@@ -11,7 +11,8 @@
 SPAN = 256
 HALF = 128
 BASE = 16
-VMEM_BYTES = 56 * 1024 * 1024
+MIB = 1024 * 1024
+STATE_MIB = 16
 
 f32 = jnp.float32
 bf16 = jnp.bfloat16
@@ -50,9 +51,26 @@
 
 
 def product_small(left, right):
-    pair = beside(*right)
-    both = dot(beside(*left), above(pair, pair))
-    return both[:, :HALF] + both[:, HALF:]
+    return dot(beside(*left), above(right[0], right[0])) + dot(left[0], right[1])
+
+
+def odd_rows(value, size):
+    return above(*(value[start : start + size] for start in range(size, value.shape[0], 2 * size)))
+
+
+def spread_rows(value, size):
+    gap = jnp.zeros((size, value.shape[1]), value.dtype)
+    return above(*(part for start in range(0, value.shape[0], size) for part in (gap, value[start : start + size])))
+
+
+def merge_rows(value, odd, size):
+    return above(
+        *(
+            part
+            for start in range(0, odd.shape[0], size)
+            for part in (value[2 * start : 2 * start + size], odd[start : start + size])
+        )
+    )
 
 
 def iotas(shape):
@@ -191,18 +209,25 @@
         for item in range(count)
     ]
     diag_parts = [split(item) for item in diag]
+    size = BASE
+    inv_parts = [split(item) for item in inverses]
     for level in range(level_ref.shape[0]):
-        mask = level_ref[level]
-        inv_parts = [split(item) for item in inverses]
+        mask = odd_rows(level_ref[level], size)
+        odd_parts = [tuple(odd_rows(part, size) for part in inv) for inv in inv_parts]
         inner = [
-            product_small((item[0] * mask, item[1] * mask), inv)
+            product_small(tuple(odd_rows(part, size) * mask for part in item), inv)
             for item, inv in zip(diag_parts, inv_parts)
         ]
-        inverses = [
-            whole - product_small(inv, split(part))
-            for whole, inv, part in zip(inverses, inv_parts, inner)
+        fresh = [
+            odd_rows(item, size) - product_small(odd, tuple(spread_rows(part, size) for part in split(part_in)))
+            for item, odd, part_in in zip(inverses, odd_parts, inner)
         ]
-    inv_parts = [split(item) for item in inverses]
+        inv_parts = [
+            tuple(merge_rows(old, new, size) for old, new in zip(inv, split(item)))
+            for inv, item in zip(inv_parts, fresh)
+        ]
+        inverses = [merge_rows(old, new, size) for old, new in zip(inverses, fresh)]
+        size *= 2
 
     right, tops, lows = [], [], []
     for head in range(heads):
@@ -268,6 +293,10 @@
         carry_out[:, head * 2 * DK : (head + 1) * 2 * DK] = beside(*split(seen[:, DV:]))
 
 
+def pack_kernel(query_ref, key_ref, val_ref, out_ref):
+    out_ref[...] = beside(query_ref[...], key_ref[...], val_ref[...])
+
+
 def compose_kernel(turn_ref, part0, part1, part2, part3, total_out, tail_out, prefix_out, all_ref):
     count = all_ref.shape[0]
     turn = turn_ref[0]
@@ -285,11 +314,16 @@
     tail_out[...] = running[:, :DV]
 
 
-def enter_kernel(turn_ref, near_ref, next_ref, far_ref, prefix_ref, out0, out1, out2, out3, all_ref):
+def enter_kernel(turn_ref, place_ref, near_ref, next_ref, far_ref, prefix_ref, out0, out1, out2, out3, all_ref):
     count = all_ref.shape[0]
     turn = turn_ref[0]
-    far = next_ref[:, :DV] + product_small(split(next_ref[:, DV:]), split(far_ref[...]))
-    entry = near_ref[:, :DV] + product_small(split(near_ref[:, DV:]), split(far))
+    place = place_ref[0]
+    near, following, far = (
+        jnp.where(place >= back, ref[...], 0.0)
+        for back, ref in ((1, near_ref), (2, next_ref), (3, far_ref))
+    )
+    far = following[:, :DV] + product_small(split(following[:, DV:]), split(far))
+    entry = near[:, :DV] + product_small(split(near[:, DV:]), split(far))
     parts = split(entry)
     all_ref[0] = entry
     for member in range(1, count):
@@ -321,8 +355,8 @@
     return pl.BlockSpec(shape, lambda *_: (0,) * len(shape))
 
 
-def params():
-    return pltpu.CompilerParams(dimension_semantics=("arbitrary",), vmem_limit_bytes=VMEM_BYTES)
+def params(mebibytes):
+    return pltpu.CompilerParams(dimension_semantics=("arbitrary",), vmem_limit_bytes=mebibytes * MIB)
 
 
 def cost(flops, size, exps=0):
@@ -338,11 +372,30 @@
     heads = value_width // DV
     spans = tok_rows // SPAN
     turn = lax.axis_index("outer").astype(jnp.int32).reshape(1)
-    tails = beside(query_in[tok_rows - 16 :], key_in[tok_rows - 16 :], value_in[tok_rows - 16 :])
+    place = lax.axis_index("inner").astype(jnp.int32).reshape(1)
+    query_far, key_in, value_in = (
+        pltpu.with_memory_space_constraint(array, pltpu.HBM) for array in (query_in, key_in, value_in)
+    )
+    tail_block = tok_rows // 16 - 1
+    all_width = 2 * query_width + value_width
+    tails = pl.pallas_call(
+        pack_kernel,
+        grid=(1,),
+        in_specs=[
+            pl.BlockSpec((16, query_width), lambda i: (tail_block, 0)),
+            pl.BlockSpec((16, query_width), lambda i: (tail_block, 0)),
+            pl.BlockSpec((16, value_width), lambda i: (tail_block, 0)),
+        ],
+        out_specs=whole((16, all_width)),
+        out_shape=jax.ShapeDtypeStruct((16, all_width), bf16),
+        compiler_params=params(4),
+        cost_estimate=cost(0, 64_000),
+        name="pack",
+    )(query_far, key_in, value_in)
     before = shifted(tails, ("inner", "outer"), 1, False)
-    query_halo = before[:, :query_width]
-    key_halo = before[:, query_width : 2 * query_width]
-    value_halo = before[:, 2 * query_width :]
+    query_halo = pl.BlockSpec((16, query_width), lambda *_: (0, 0))
+    key_halo = pl.BlockSpec((16, query_width), lambda *_: (0, 1))
+    value_halo = pl.BlockSpec((16, value_width), lambda *_: (0, 2 * query_width // value_width))
     gates = above(log_decay.T, beta_gate.T)
 
     def prev_rows(offset):
@@ -357,10 +410,10 @@
             in_specs=[
                 pl.BlockSpec((SPAN, query_width), lambda i, *_: (i, 0)),
                 pl.BlockSpec((16, query_width), prev_rows(0)),
-                whole((16, query_width)),
+                key_halo,
                 pl.BlockSpec((SPAN, value_width), lambda i, *_: (i, 0)),
                 pl.BlockSpec((16, value_width), prev_rows(0)),
-                whole((16, value_width)),
+                value_halo,
                 pl.BlockSpec((2 * heads, SPAN), lambda i, *_: (0, i)),
                 whole((CONV, query_width)),
                 whole((CONV, value_width)),
@@ -391,10 +444,10 @@
             jax.ShapeDtypeStruct((tok_rows, HALF), f32),
         ]
         + [square] * 4,
-        compiler_params=params(),
+        compiler_params=params(STATE_MIB),
         cost_estimate=cost(20_000_000_000, 20_000_000),
         name="state_path",
-    )(turn, key_in, key_in, key_halo, value_in, value_in, value_halo, gates, conv_key, conv_value)
+    )(turn, key_in, key_in, before, value_in, value_in, before, gates, conv_key, conv_value)
 
     parts = [ends[0]] + [shifted(ends[k], "outer", k, True) for k in (1, 2, 3)]
 
@@ -416,7 +469,7 @@
             in_specs=[
                 pl.BlockSpec((SPAN, query_width), lambda i: (at(i), 0)),
                 pl.BlockSpec((16, query_width), prev_rows(offset)),
-                whole((16, query_width)),
+                query_halo,
                 whole((CONV, query_width)),
                 pl.BlockSpec((1, key_heads, 2, DK, SPAN), lambda i: (at(i), 0, 0, 0, 0)),
                 pl.BlockSpec((1, heads, 2, SPAN, 2 * DV), lambda i: (at(i), 0, 0, 0, 0)),
@@ -431,12 +484,14 @@
             ],
             out_shape=out_types,
             input_output_aliases={9 + k: k for k in range(len(earlier))},
-            compiler_params=params(),
+            compiler_params=params(14),
             cost_estimate=cost(2_000_000_000 * count, 3_000_000 * count),
             name="query_path",
-        )(query_in, query_in, query_halo, conv_query, keyt, solved, starts, rows, cols, *earlier)
-
-    first_half = query_part(0, spans // 2, ())
+        )(query_in, query_in, before, conv_query, keyt, solved, starts, rows, cols, *earlier)
+
+    cuts = (0, (3 * spans) // 8, (6 * spans) // 8, spans)
+    seen = query_part(cuts[0], cuts[1] - cuts[0], ())
+    parts, seen = lax.optimization_barrier((parts, seen))
 
     total, tail, prefix = pl.pallas_call(
         compose_kernel,
@@ -452,30 +507,32 @@
             jax.ShapeDtypeStruct((DK, DV), f32),
             jax.ShapeDtypeStruct((3, DK, 2 * DV), f32),
         ],
-        compiler_params=params(),
+        compiler_params=params(8),
         cost_estimate=cost(100_000_000, 1_000_000),
         name="compose",
     )(turn, *parts)
-    near = shifted(total, "inner", 1, False)
-    middle = shifted(total, "inner", 2, False)
-    far = shifted(tail, "inner", 3, False)
-
-    local, carry = query_part(spans // 2, spans - spans // 2, first_half)
+    near = shifted(total, "inner", 1, True)
+    middle = shifted(total, "inner", 2, True)
+    far = shifted(tail, "inner", 3, True)
+
+    seen = query_part(cuts[1], cuts[2] - cuts[1], seen)
+    near, seen = lax.optimization_barrier((near, seen))
+    local, carry = query_part(cuts[2], cuts[3] - cuts[2], seen)
 
     entries = pl.pallas_call(
         enter_kernel,
         grid_spec=pltpu.PrefetchScalarGridSpec(
-            num_scalar_prefetch=1,
+            num_scalar_prefetch=2,
             grid=(1,),
             in_specs=[whole((DK, 2 * DV)), whole((DK, 2 * DV)), whole((DK, DV)), whole((3, DK, 2 * DV))],
             out_specs=[whole((DK, DV))] * 4,
             scratch_shapes=[pltpu.VMEM((4, DK, DV), f32)],
         ),
         out_shape=[jax.ShapeDtypeStruct((DK, DV), f32)] * 4,
-        compiler_params=params(),
+        compiler_params=params(8),
         cost_estimate=cost(50_000_000, 1_000_000),
         name="enter",
-    )(turn, near, middle, far, prefix)
+    )(turn, place, near, middle, far, prefix)
     states = [entries[0]] + [shifted(entries[k], "outer", k, True) for k in (1, 2, 3)]
 
     return pl.pallas_call(
@@ -493,7 +550,7 @@
             scratch_shapes=[pltpu.VMEM((heads, 2 * DK, 2 * DV), bf16)],
         ),
         out_shape=jax.ShapeDtypeStruct((tok_rows, value_width), bf16),
-        compiler_params=params(),
+        compiler_params=params(10),
         cost_estimate=cost(2_000_000_000, 10_000_000),
         name="close",
     )(turn, *states, local, carry, norm_gain.reshape(1, value_width))

time: 98.6 us -> 70.4 us (0.71)
  Pallas kernels: 62.3 us -> 44.6 us
  local copies, waits for them, and re-layouts: 5.32 us -> 0.03 us
  starting transfers between devices: 24.3 us -> 22 us
  other arithmetic: 1.43 us -> 0.02 us
    pallas_call x2 -> x3, Pallas kernels: 16.4 us -> 9.5 us  [query_part(): pl.pallas_call(body, grid=(count,), in_specs=[pl.BlockSpec((SPAN, query_w...]
    pallas_call x1, Pallas kernels: 32.6 us -> 28.2 us  [per_device(): pl.pallas_call(state_kernel, grid_spec=pltpu.PrefetchScalarGridSpec(num_s...]
    pallas_call x1, Pallas kernels: 8.33 us -> 4.88 us  [per_device(): pl.pallas_call(close_kernel, grid_spec=pltpu.PrefetchScalarGridSpec(num_s...]
    slice x5 -> x0, local copies, waits for them, and re-layouts: 3.32 us -> none  [the longest x1 0.72 us: per_device(): value_in[tok_rows - 16:]]
    ppermute x10, starting transfers between devices: 24.3 us -> 22 us  [shifted(): return lax.ppermute(value, axis, pairs)]
    unnamed x18 -> x14, local copies, waits for them, and re-layouts: 2 us -> 0.03 us
    pallas_call x1, Pallas kernels: 2.57 us -> 0.61 us  [per_device(): pl.pallas_call(compose_kernel, grid_spec=pltpu.PrefetchScalarGridSpec(num...]
    pallas_call x1, Pallas kernels: 2.46 us -> 0.62 us  [per_device(): pl.pallas_call(enter_kernel, grid_spec=pltpu.PrefetchScalarGridSpec(num_s...]
  transfers between devices with their start and end apart: 10 -> 10, of which waited for: 4 -> 3; matrix products, arithmetic and copies ran while one was open for 1% -> 0% of each run, Pallas kernels for 17% -> 14%
where the time goes in v2:
time: 70.4 us; the launch traced here: 70.2 us
  Pallas kernels  44.6 us (63%)
  starting transfers between devices  22 us (31%)
  waiting for transfers between devices  3.44 us (5%)
    pallas_call x1, Pallas kernels, per_device(): pl.pallas_call(state_kernel, grid_spec=pltpu.PrefetchScalarGridSpec(num_s...  28.2 us
    ppermute x10, starting transfers between devices, shifted(): return lax.ppermute(value, axis, pairs)  22 us
    pallas_call x3, Pallas kernels, query_part(): pl.pallas_call(body, grid=(count,), in_specs=[pl.BlockSpec((SPAN, query_w...  9.5 us
    pallas_call x1, Pallas kernels, per_device(): pl.pallas_call(close_kernel, grid_spec=pltpu.PrefetchScalarGridSpec(num_s...  4.88 us
    ppermute x10, waiting for transfers between devices, shifted(): return lax.ppermute(value, axis, pairs)  3.44 us
  transfers between devices with their start and end apart: 10, of which 3 were waited for; matrix products, arithmetic and copies ran while one was open for 0% of the time, Pallas kernels for 14%

profile of v2, /device:TPU:0, one launch (start us, length us, event | category | flops | bytes accessed | tf_op | source)
XLA Modules:
  0.0 70.2 jit_solution(3343077589129203914)
XLA Ops:
  0.0 0.8 %pack.1 = bf16[16,1024]{1,0:T(8,128)(2,1)S(1)} custom-call(bf16[2048,256]{1,0:T(8,128)(2,1)} %refs_1_.5, bf16[2048,256]{1,0:T(8,128)(2,1)} %key_prev.1, bf16[2048,512]{1,0:T(8,128)(2,1)} %val_prev.1), custom_call_target="tpu_custom_call" | custom-call | bytes 64000 | tf_op jit(solution)/shard_map/pack/pallas_call | solution.py:381
  0.8 3.6 %collective-permute-start = (bf16[16,1024]{1,0:T(8,128)(2,1)S(1)}, bf16[16,1024]{1,0:T(8,128)(2,1)S(1)}, u32[]{:S(2)}, u32[]{:S(2)}) collective-permute-start(bf16[16,1024]{1,0:T(8,128)(2,1)S(1)} %pack.1), channel_id=1, source_target_pairs={{0,1},{1,2},{2,3},{3,4},{4,5},{5,6},{6,7},{7,8},{8,9},{9,10},{10,1... | collective-permute-start | bytes 98312 | tf_op jit(solution)/shard_map/ppermute | solution.py:27
  4.4 0.0 copy-done.5
  4.4 0.0 copy-done.6
  4.4 1.5 %collective-permute-done.key_halo.val_halo.refs_2_ = bf16[16,1024]{1,0:T(8,128)(2,1)S(1)} collective-permute-done((bf16[16,1024]{1,0:T(8,128)(2,1)S(1)}, bf16[16,1024]{1,0:T(8,128)(2,1)S(1)}, u32[]{:S(2)}, u32[]{:S(2)}) %collective-permute-start) | collective-permute-done | bytes 32800 | tf_op jit(solution)/shard_map/ppermute | solution.py:27
  6.0 0.0 copy-done.4
  6.0 28.2 %state_path.1 = (bf16[8,2,2,128,256]{4,3,2,1,0:T(8,128)(2,1)S(1)}, bf16[8,4,2,256,256]{4,3,2,1,0:T(8,128)(2,1)S(1)}, bf16[8,4,2,128,256]{4,3,2,1,0:T(8,128)(2,1)...) custom-call(s32[1]{0:T(128)} %bitcast.turn_ref, ...), custom_call_target="tpu_custom_call" | custom-call | flops 20000000000 | bytes 20000000 | tf_op jit(solution)/shard_map/state_path/pallas_call | solution.py:405
  34.2 2.4 %collective-permute-start.1 = (f32[128,256]{1,0:T(8,128)S(1)}, f32[128,256]{1,0:T(8,128)S(1)}, u32[]{:S(2)}, u32[]{:S(2)}) collective-permute-start(f32[128,256]{1,0:T(8,128)S(1)} %get-tuple-element.37), channel_id=1, source_target_pairs={{0,1},{1,2},{2,3},{3,0},{4,5},{5,6},{6,7},{7,4},{8,9},{9,10},{10,1... | collective-permute-start | bytes 393224 | tf_op jit(solution)/shard_map/ppermute | solution.py:27
  36.5 2.9 %collective-permute-start.2 = (f32[128,256]{1,0:T(8,128)S(1)}, f32[128,256]{1,0:T(8,128)S(1)}, u32[]{:S(2)}, u32[]{:S(2)}) collective-permute-start(f32[128,256]{1,0:T(8,128)S(1)} %get-tuple-element.38), channel_id=1, source_target_pairs={{0,2},{1,3},{2,0},{3,1},{4,6},{5,7},{6,4},{7,5},{8,10},{9,11},{10,... | collective-permute-start | bytes 393224 | tf_op jit(solution)/shard_map/ppermute | solution.py:27
  39.5 1.3 %collective-permute-start.3 = (f32[128,256]{1,0:T(8,128)S(1)}, f32[128,256]{1,0:T(8,128)S(1)}, u32[]{:S(2)}, u32[]{:S(2)}) collective-permute-start(f32[128,256]{1,0:T(8,128)S(1)} %get-tuple-element.39), channel_id=1, source_target_pairs={{0,3},{1,0},{2,1},{3,2},{4,7},{5,4},{6,5},{7,6},{8,11},{9,8},{10,9... | collective-permute-start | bytes 393224 | tf_op jit(solution)/shard_map/ppermute | solution.py:27
  40.8 3.6 %query_path.3 = (f32[2048,512]{1,0:T(8,128)S(1)}, bf16[2048,1024]{1,0:T(8,128)(2,1)S(1)}) custom-call(bf16[2048,256]{1,0:T(8,128)(2,1)S(1)} %copy-done, bf16[2048,256]{1,0:T(8,128)(2,1)S(1)} %copy-done, bf16[16,1024]{1,0:T(8,128)(2,1)S(1)} %collective-permute-done.key_halo.val_halo.refs_2_, bf16[4,256]{1,0:T(4,128)(2,1)S(1)} %copy-done.1, ...), custom_call_target="tpu_custom_call" | custom-call | flops 6000000000 | bytes 9000000 | tf_op jit(solution)/shard_map/query_path/pallas_call | solution.py:466
  44.4 0.0 collective-permute-done.1.part1
  44.4 0.0 collective-permute-done.2.part2
  44.4 0.0 collective-permute-done.3.part3
  44.4 0.6 compose.1
  45.0 4.5 %collective-permute-start.5 = (f32[128,256]{1,0:T(8,128)S(1)}, f32[128,256]{1,0:T(8,128)S(1)}, u32[]{:S(2)}, u32[]{:S(2)}) collective-permute-start(f32[128,256]{1,0:T(8,128)S(1)} %get-tuple-element.51), channel_id=1, source_target_pairs={{0,8},{4,12},{8,0},{12,4},{1,9},{5,13},{9,1},{13,5},{2,10},{6,14},... | collective-permute-start | bytes 393224 | tf_op jit(solution)/shard_map/ppermute | solution.py:27
  49.6 0.6 collective-permute-start.4
  50.2 2.6 %collective-permute-start.6 = (f32[128,128]{1,0:T(8,128)S(1)}, f32[128,128]{1,0:T(8,128)S(1)}, u32[]{:S(2)}, u32[]{:S(2)}) collective-permute-start(f32[128,128]{1,0:T(8,128)S(1)} %get-tuple-element.57), channel_id=1, source_target_pairs={{0,12},{4,0},{8,4},{12,8},{1,13},{5,1},{9,5},{13,9},{2,14},{6,2},{... | collective-permute-start | bytes 196616 | tf_op jit(solution)/shard_map/ppermute | solution.py:27
  52.8 3.6 %query_path.4 = (f32[2048,512]{1,0:T(8,128)S(1)}, bf16[2048,1024]{1,0:T(8,128)(2,1)S(1)}) custom-call(bf16[2048,256]{1,0:T(8,128)(2,1)S(1)} %copy-done, bf16[2048,256]{1,0:T(8,128)(2,1)S(1)} %copy-done, bf16[16,1024]{1,0:T(8,128)(2,1)S(1)} %collective-permute-done.key_halo.val_halo.refs_2_, ...), custom_call_target="tpu_custom_call", output_to_operand_aliasing={{0}: (9, {}), {1}: (10, {})} | custom-call | flops 6000000000 | bytes 9000000 | tf_op jit(solution)/shard_map/query_path/pallas_call | solution.py:466
  56.4 0.0 collective-permute-done.4.near_ref
  56.4 0.0 collective-permute-done.6.far_ref
  56.4 0.0 collective-permute-done.5.next_ref
  56.4 0.6 enter.1
  57.0 0.5 collective-permute-start.7
  57.5 3.6 %collective-permute-start.8 = (f32[128,128]{1,0:T(8,128)S(1)}, f32[128,128]{1,0:T(8,128)S(1)}, u32[]{:S(2)}, u32[]{:S(2)}) collective-permute-start(f32[128,128]{1,0:T(8,128)S(1)} %get-tuple-element.61), channel_id=1, source_target_pairs={{0,2},{1,3},{2,0},{3,1},{4,6},{5,7},{6,4},{7,5},{8,10},{9,11},{10,... | collective-permute-start | bytes 196616 | tf_op jit(solution)/shard_map/ppermute | solution.py:27
  61.1 0.0 collective-permute-start.9
  61.1 2.4 %query_path.5 = (f32[2048,512]{1,0:T(8,128)S(1)}, bf16[2048,1024]{1,0:T(8,128)(2,1)S(1)}) custom-call(bf16[2048,256]{1,0:T(8,128)(2,1)S(1)} %copy-done, bf16[2048,256]{1,0:T(8,128)(2,1)S(1)} %copy-done, bf16[16,1024]{1,0:T(8,128)(2,1)S(1)} %collective-permute-done.key_halo.val_halo.refs_2_, ...), custom_call_target="tpu_custom_call", output_to_operand_aliasing={{0}: (9, {}), {1}: (10, {})} | custom-call | flops 4000000000 | bytes 6000000 | tf_op jit(solution)/shard_map/query_path/pallas_call | solution.py:466
  63.5 0.0 collective-permute-done.7.part1
  63.5 0.5 collective-permute-done.8.part2
  64.0 1.3 %collective-permute-done.9.part3 = f32[128,128]{1,0:T(8,128)S(1)} collective-permute-done((f32[128,128]{1,0:T(8,128)S(1)}, f32[128,128]{1,0:T(8,128)S(1)}, u32[]{:S(2)}, u32[]{:S(2)}) %collective-permute-start.9) | collective-permute-done | bytes 65568 | tf_op jit(solution)/shard_map/ppermute | solution.py:27
  65.3 0.0 copy-done.2
  65.3 4.9 %close.1 = bf16[2048,512]{1,0:T(8,128)(2,1)} custom-call(s32[1]{0:T(128)} %bitcast.turn_ref, f32[128,128]{1,0:T(8,128)S(1)} %get-tuple-element.59.part0, f32[128,128]{1,0:T(8,128)S(1)} %collective-permute-done.7.part1, f32[128,128]{1,0:T(8,128)S(1)} %collective-permute-done.8.part2, f32[128,128]{1,0:T(8,128)S(1)} %collective-permute-done.9.part3, ...), custom_call_target="tpu_custom_call" | custom-call | flops 2000000000 | bytes 10000000 | tf_op jit(solution)/shard_map/close/pallas_call | solution.py:538
  (11 shorter events, 0.0 us)
Async XLA Ops:
  0.0 4.4 %copy-start.5 = (f32[2048,4]{0,1:T(4,128)S(1)}, f32[2048,4]{0,1:T(4,128)}, u32[]{:S(2)}) copy-start(f32[2048,4]{0,1:T(4,128)} %param.13) | copy-start | bytes 98308
  0.0 4.4 %copy-start.6 = (f32[2048,4]{0,1:T(4,128)S(1)}, f32[2048,4]{0,1:T(4,128)}, u32[]{:S(2)}) copy-start(f32[2048,4]{0,1:T(4,128)} %param.12) | copy-start | bytes 98308
  0.0 6.0 %copy-start.3 = (bf16[4,512]{1,0:T(4,128)(2,1)S(1)}, bf16[4,512]{1,0:T(4,128)(2,1)}, u32[]{:S(2)}) copy-start(bf16[4,512]{1,0:T(4,128)(2,1)} %val_taps.1) | copy-start | bytes 12292
  0.0 6.0 %copy-start.4 = (bf16[4,256]{1,0:T(4,128)(2,1)S(1)}, bf16[4,256]{1,0:T(4,128)(2,1)}, u32[]{:S(2)}) copy-start(bf16[4,256]{1,0:T(4,128)(2,1)} %key_taps.1) | copy-start | bytes 6148
  0.8 5.2 %collective-permute-start = (bf16[16,1024]{1,0:T(8,128)(2,1)S(1)}, bf16[16,1024]{1,0:T(8,128)(2,1)S(1)}, u32[]{:S(2)}, u32[]{:S(2)}) collective-permute-start(bf16[16,1024]{1,0:T(8,128)(2,1)S(1)} %pack.1), channel_id=1, source_target_pairs={{0,1},{1,2},{2,3},{3,4},{4,5},{5,6},{6,7},{7,8},{8,9},{9,10},{10,1... | collective-permute-start | bytes 98312 | tf_op jit(solution)/shard_map/ppermute | solution.py:27
  6.0 34.8 %copy-start = (bf16[2048,256]{1,0:T(8,128)(2,1)S(1)}, bf16[2048,256]{1,0:T(8,128)(2,1)}, u32[]{:S(2)}) copy-start(bf16[2048,256]{1,0:T(8,128)(2,1)} %refs_1_.5) | copy-start | bytes 3145732
  6.0 34.8 %copy-start.1 = (bf16[4,256]{1,0:T(4,128)(2,1)S(1)}, bf16[4,256]{1,0:T(4,128)(2,1)}, u32[]{:S(2)}) copy-start(bf16[4,256]{1,0:T(4,128)(2,1)} %refs_3_.5) | copy-start | bytes 6148
  34.2 10.2 %collective-permute-start.1 = (f32[128,256]{1,0:T(8,128)S(1)}, f32[128,256]{1,0:T(8,128)S(1)}, u32[]{:S(2)}, u32[]{:S(2)}) collective-permute-start(f32[128,256]{1,0:T(8,128)S(1)} %get-tuple-element.37), channel_id=1, source_target_pairs={{0,1},{1,2},{2,3},{3,0},{4,5},{5,6},{6,7},{7,4},{8,9},{9,10},{10,1... | collective-permute-start | bytes 393224 | tf_op jit(solution)/shard_map/ppermute | solution.py:27
  36.5 7.8 %collective-permute-start.2 = (f32[128,256]{1,0:T(8,128)S(1)}, f32[128,256]{1,0:T(8,128)S(1)}, u32[]{:S(2)}, u32[]{:S(2)}) collective-permute-start(f32[128,256]{1,0:T(8,128)S(1)} %get-tuple-element.38), channel_id=1, source_target_pairs={{0,2},{1,3},{2,0},{3,1},{4,6},{5,7},{6,4},{7,5},{8,10},{9,11},{10,... | collective-permute-start | bytes 393224 | tf_op jit(solution)/shard_map/ppermute | solution.py:27
  39.5 5.0 %collective-permute-start.3 = (f32[128,256]{1,0:T(8,128)S(1)}, f32[128,256]{1,0:T(8,128)S(1)}, u32[]{:S(2)}, u32[]{:S(2)}) collective-permute-start(f32[128,256]{1,0:T(8,128)S(1)} %get-tuple-element.39), channel_id=1, source_target_pairs={{0,3},{1,0},{2,1},{3,2},{4,7},{5,4},{6,5},{7,6},{8,11},{9,8},{10,9... | collective-permute-start | bytes 393224 | tf_op jit(solution)/shard_map/ppermute | solution.py:27
  45.0 11.4 %collective-permute-start.5 = (f32[128,256]{1,0:T(8,128)S(1)}, f32[128,256]{1,0:T(8,128)S(1)}, u32[]{:S(2)}, u32[]{:S(2)}) collective-permute-start(f32[128,256]{1,0:T(8,128)S(1)} %get-tuple-element.51), channel_id=1, source_target_pairs={{0,8},{4,12},{8,0},{12,4},{1,9},{5,13},{9,1},{13,5},{2,10},{6,14},... | collective-permute-start | bytes 393224 | tf_op jit(solution)/shard_map/ppermute | solution.py:27
  49.6 6.8 %collective-permute-start.4 = (f32[128,256]{1,0:T(8,128)S(1)}, f32[128,256]{1,0:T(8,128)S(1)}, u32[]{:S(2)}, u32[]{:S(2)}) collective-permute-start(f32[128,256]{1,0:T(8,128)S(1)} %get-tuple-element.51), channel_id=1, source_target_pairs={{0,4},{4,8},{8,12},{12,0},{1,5},{5,9},{9,13},{13,1},{2,6},{6,10},{... | collective-permute-start | bytes 393224 | tf_op jit(solution)/shard_map/ppermute | solution.py:27
  50.2 6.2 %collective-permute-start.6 = (f32[128,128]{1,0:T(8,128)S(1)}, f32[128,128]{1,0:T(8,128)S(1)}, u32[]{:S(2)}, u32[]{:S(2)}) collective-permute-start(f32[128,128]{1,0:T(8,128)S(1)} %get-tuple-element.57), channel_id=1, source_target_pairs={{0,12},{4,0},{8,4},{12,8},{1,13},{5,1},{9,5},{13,9},{2,14},{6,2},{... | collective-permute-start | bytes 196616 | tf_op jit(solution)/shard_map/ppermute | solution.py:27
  57.0 6.4 %collective-permute-start.7 = (f32[128,128]{1,0:T(8,128)S(1)}, f32[128,128]{1,0:T(8,128)S(1)}, u32[]{:S(2)}, u32[]{:S(2)}) collective-permute-start(f32[128,128]{1,0:T(8,128)S(1)} %get-tuple-element.60), channel_id=1, source_target_pairs={{0,1},{1,2},{2,3},{3,0},{4,5},{5,6},{6,7},{7,4},{8,9},{9,10},{10,1... | collective-permute-start | bytes 196616 | tf_op jit(solution)/shard_map/ppermute | solution.py:27
  57.5 6.5 %collective-permute-start.8 = (f32[128,128]{1,0:T(8,128)S(1)}, f32[128,128]{1,0:T(8,128)S(1)}, u32[]{:S(2)}, u32[]{:S(2)}) collective-permute-start(f32[128,128]{1,0:T(8,128)S(1)} %get-tuple-element.61), channel_id=1, source_target_pairs={{0,2},{1,3},{2,0},{3,1},{4,6},{5,7},{6,4},{7,5},{8,10},{9,11},{10,... | collective-permute-start | bytes 196616 | tf_op jit(solution)/shard_map/ppermute | solution.py:27
  61.1 4.3 %copy-start.2 = (f32[512]{0:T(512)S(1)}, f32[512]{0:T(512)}, u32[]{:S(2)}) copy-start(f32[512]{0:T(512)} %param.17) | copy-start | bytes 6148
  61.1 4.3 %collective-permute-start.9 = (f32[128,128]{1,0:T(8,128)S(1)}, f32[128,128]{1,0:T(8,128)S(1)}, u32[]{:S(2)}, u32[]{:S(2)}) collective-permute-start(f32[128,128]{1,0:T(8,128)S(1)} %get-tuple-element.62), channel_id=1, source_target_pairs={{0,3},{1,0},{2,1},{3,2},{4,7},{5,4},{6,5},{7,6},{8,11},{9,8},{10,9... | collective-permute-start | bytes 196616 | tf_op jit(solution)/shard_map/ppermute | solution.py:27

commit v3 on v2

v3 whole, which is shorter than its diff:
```python
import jax
import jax.numpy as jnp
from jax import lax
from jax.experimental import pallas as pl
from jax.experimental.pallas import tpu as pltpu
from jax.sharding import PartitionSpec as P

DK = 128
DV = 128
CONV = 4
SPAN = 256
HALF = 128
BASE = 16
MIB = 1024 * 1024
STATE_MIB = 16
QUERY_MIB = 14

f32 = jnp.float32
bf16 = jnp.bfloat16


def shifted(value, axis, steps, wrap):
    count = lax.axis_size(axis)
    if wrap:
        pairs = [(source, (source + steps) % count) for source in range(count)]
    else:
        pairs = [(source, source + steps) for source in range(count - steps)]
    return lax.ppermute(value, axis, pairs)


def split(value):
    high = value.astype(bf16)
    return high, (value - high.astype(f32)).astype(bf16)


def dot(left, right):
    return jnp.dot(left, right, preferred_element_type=f32)


def beside(*parts):
    return jnp.concatenate(parts, axis=1)


def above(*parts):
    return jnp.concatenate(parts, axis=0)


def product(left, right):
    if left[0].shape[1] == HALF:
        return dot(beside(*left), above(right[0], right[0])) + dot(left[0], right[1])
    return dot(left[0], right[0]) + dot(left[1], right[0]) + dot(left[0], right[1])


def product_small(left, right):
    return dot(beside(*left), above(right[0], right[0])) + dot(left[0], right[1])


def odd_rows(value, size):
    return above(*(value[start : start + size] for start in range(size, value.shape[0], 2 * size)))


def spread_rows(value, size):
    gap = jnp.zeros((size, value.shape[1]), value.dtype)
    return above(*(part for start in range(0, value.shape[0], size) for part in (gap, value[start : start + size])))


def merge_rows(value, odd, size):
    return above(
        *(
            part
            for start in range(0, odd.shape[0], size)
            for part in (value[2 * start : 2 * start + size], odd[start : start + size])
        )
    )


def iotas(shape):
    return lax.broadcasted_iota(jnp.int32, shape, 0), lax.broadcasted_iota(jnp.int32, shape, 1)


def conv_silu(halo, prev, cur, taps, first):
    prev = jnp.where(first, halo.astype(f32), prev.astype(f32))
    cur = cur.astype(f32)
    taps = taps.astype(f32)
    extended = above(prev[8:], cur)
    rows = cur.shape[0]
    total = taps[CONV - 1 : CONV] * cur
    for tap in range(CONV - 1):
        start = 8 - (CONV - 1) + tap
        total = total + taps[tap : tap + 1] * extended[start : start + rows]
    return total / (1.0 + jnp.exp(-total))


def decay_blocks(cum_col, cum_row, strict):
    row_ids, col_ids = iotas((HALF, HALF))
    keep = (row_ids > col_ids) if strict else (row_ids >= col_ids)
    top = jnp.exp(jnp.where(keep, cum_col[:HALF] - cum_row[:, :HALF], -1e30))
    low = jnp.exp(cum_col[HALF:] - cum_row[:, :HALF])
    end = jnp.exp(jnp.where(keep, cum_col[HALF:] - cum_row[:, HALF:], -1e30))
    return top, low, end


def state_kernel(
    turn_ref, halo_ref, key_ref, val_ref, gate_ref, key_taps, val_taps,
    keyt_out, solved_out, start_out, row_out, col_out, end0, end1, end2, end3,
    run_ref, map_ref, add_ref, fin_ref, level_ref, pick_ref, tri_ref,
    inv_ref, below_ref, keyed_ref, turned_ref, feat_ref, held_ref, cum_ref,
):
    heads = run_ref.shape[0]
    width = key_ref.shape[1]
    key_heads = width // DK
    spans = key_ref.shape[0] // SPAN
    halo = halo_ref[...]
    group = heads // key_heads
    row_ids, col_ids = iotas((HALF, HALF))
    unit = jnp.where(row_ids == col_ids, 1.0, 0.0).astype(f32)
    base_mask = (row_ids // BASE) == (col_ids // BASE)

    zeros = jnp.zeros((HALF, HALF), f32)
    for head in range(heads):
        run_ref[head, 0] = beside(zeros, unit).astype(bf16)
        run_ref[head, 1] = beside(zeros, zeros).astype(bf16)
        map_ref[head] = beside(unit, zeros).astype(bf16)
        add_ref[head] = zeros
    size = BASE
    for level in range(level_ref.shape[0]):
        picked = (
            (row_ids // (2 * size) == col_ids // (2 * size))
            & (row_ids % (2 * size) >= size)
            & (col_ids % (2 * size) < size)
        )
        level_ref[level] = jnp.where(picked, 1.0, 0.0).astype(bf16)
        size *= 2
    for place in range(BASE - 1):
        chosen = jnp.where(row_ids == (col_ids // BASE) * BASE + place, 1.0, 0.0).astype(bf16)
        pick_ref[:, place * HALF : (place + 1) * HALF] = above(chosen, chosen)
    tri_rows, tri_cols = iotas((SPAN, SPAN))
    tri_ref[...] = jnp.where(tri_rows <= tri_cols, 1.0, 0.0).astype(bf16)
    for ref in (inv_ref, below_ref, keyed_ref, turned_ref, feat_ref, held_ref, cum_ref):
        ref[...] = jnp.zeros(ref.shape, ref.dtype)

    def advance(head):
        maps = map_ref[head]
        high, low = run_ref[head, 0], run_ref[head, 1]
        moved = dot(maps, above(high, high)) + dot(maps[:, :DK], low)
        return beside(moved[:, :DV] + add_ref[head], moved[:, DV:])

    def follow(span):
        for head in range(heads):
            high, low = split(advance(head))
            run_ref[head, 0] = high
            run_ref[head, 1] = low
            start_out[span, head, 0] = high
            start_out[span, head, 1] = low

    def prepare(span):
        rows_at = pl.multiple_of(span * SPAN, SPAN)
        here = pl.ds(rows_at, SPAN)
        ahead = pl.ds(pl.multiple_of(jnp.maximum(rows_at - 16, 0), 16), 16)
        gates = gate_ref[:, here]
        is_log = lax.broadcasted_iota(jnp.int32, gates.shape, 0) < heads
        logs = jnp.where(is_log, gates, 0.0)
        logs = above(logs, logs)
        high = logs.astype(bf16)
        rest = logs - high.astype(f32)
        mid = rest.astype(bf16)
        low = (rest - mid.astype(f32)).astype(bf16)
        tri = tri_ref[...]
        cum = (dot(high, tri) + dot(mid, tri) + dot(low, tri))[: gates.shape[0]]
        row_out[:, here] = cum
        packed = above(
            jnp.where(is_log, cum, gates),
            jnp.exp(cum),
            jnp.zeros((HALF - 2 * gates.shape[0], SPAN), f32),
        )
        cols = packed.T
        col_out[here, :] = cols

        first = span == 0
        key_feat = conv_silu(halo[:, width : 2 * width], key_ref[ahead, :], key_ref[here, :], key_taps[...], first)
        val_feat = conv_silu(halo[:, 2 * width :], val_ref[ahead, :], val_ref[here, :], val_taps[...], first)

        keys, keys_t, grams = [], [], []
        for key_head in range(key_heads):
            feat = key_feat[:, key_head * DK : (key_head + 1) * DK]
            keyed = feat * lax.rsqrt(jnp.sum(feat * feat, axis=1, keepdims=True) + 1e-6)
            turned = keyed.T
            parts = split(turned)
            keyt_out[span, key_head, 0] = parts[0]
            keyt_out[span, key_head, 1] = parts[1]
            keys.append(keyed)
            keys_t.append(turned)
            grams.append(product(split(keyed), parts))

        diag, below = [], []
        for head in range(heads):
            gram = grams[head // group]
            beta_col = cols[:, heads + head : heads + head + 1]
            top, low, end = decay_blocks(cols[:, head : head + 1], cum[head : head + 1], True)
            diag.append(gram[:HALF, :HALF] * top * beta_col[:HALF])
            below.append(split(gram[HALF:, :HALF] * low * beta_col[HALF:]))
            diag.append(gram[HALF:, HALF:] * end * beta_col[HALF:])

        blocks = HALF // BASE
        compact = above(
            *(jnp.sum(jnp.where(base_mask, item, 0.0).reshape(blocks, BASE, HALF), axis=0) for item in diag)
        )
        spread = dot(beside(*split(compact)), pick_ref[...])
        count = len(diag)
        within = lax.broadcasted_iota(jnp.int32, (count, BASE, HALF), 1)
        lanes = lax.broadcasted_iota(jnp.int32, (count, BASE, HALF), 2)
        small = jnp.where(within == lanes % BASE, 1.0, 0.0).astype(f32)
        for place in range(BASE - 1):
            factor = spread[:, place * HALF : (place + 1) * HALF].reshape(count, BASE, HALF)
            small = small - factor * small[:, place : place + 1, :]
        inverses = [
            jnp.where(base_mask, jnp.broadcast_to(small[item][None], (blocks, BASE, HALF)).reshape(HALF, HALF), 0.0)
            for item in range(count)
        ]
        diag_parts = [split(item) for item in diag]
        size = BASE
        inv_parts = [split(item) for item in inverses]
        for level in range(level_ref.shape[0]):
            mask = odd_rows(level_ref[level], size)
            odd_parts = [tuple(odd_rows(part, size) for part in inv) for inv in inv_parts]
            inner = [
                product_small(tuple(odd_rows(part, size) * mask for part in item), inv)
                for item, inv in zip(diag_parts, inv_parts)
            ]
            fresh = [
                odd_rows(item, size) - product_small(odd, tuple(spread_rows(part, size) for part in split(part_in)))
                for item, odd, part_in in zip(inverses, odd_parts, inner)
            ]
            inv_parts = [
                tuple(merge_rows(old, new, size) for old, new in zip(inv, split(item)))
                for inv, item in zip(inv_parts, fresh)
            ]
            inverses = [merge_rows(old, new, size) for old, new in zip(inverses, fresh)]
            size *= 2

        for item in range(count):
            inv_ref[item, 0], inv_ref[item, 1] = inv_parts[item]
        for head in range(heads):
            below_ref[head, 0], below_ref[head, 1] = below[head]
        for key_head in range(key_heads):
            keyed_ref[key_head] = keys[key_head]
            turned_ref[key_head] = keys_t[key_head]
        feat_ref[...] = val_feat
        held_ref[...] = cols
        cum_ref[...] = cum

    def solve(span):
        inv_parts = [(inv_ref[item, 0], inv_ref[item, 1]) for item in range(2 * heads)]
        below = [(below_ref[head, 0], below_ref[head, 1]) for head in range(heads)]
        keys = [keyed_ref[key_head] for key_head in range(key_heads)]
        keys_t = [turned_ref[key_head] for key_head in range(key_heads)]
        val_feat, cols, cum = feat_ref[...], held_ref[...], cum_ref[...]
        right, tops, lows = [], [], []
        for head in range(heads):
            beta_col = cols[:, heads + head : heads + head + 1]
            exp_col = cols[:, 2 * heads + head : 2 * heads + head + 1]
            right.append(
                beside(keys[head // group] * (beta_col * exp_col), val_feat[:, head * DV : (head + 1) * DV] * beta_col)
            )
        for head in range(heads):
            tops.append(split(product(inv_parts[2 * head], split(right[head][:HALF]))))
        for head in range(heads):
            rest = right[head][HALF:] - product(below[head], tops[head])
            lows.append(split(product(inv_parts[2 * head + 1], split(rest))))
        for head in range(heads):
            solved = (above(tops[head][0], lows[head][0]), above(tops[head][1], lows[head][1]))
            solved_out[span, head, 0] = solved[0]
            solved_out[span, head, 1] = solved[1]
            cum_row = cum[head : head + 1]
            last = cum_row[:, SPAN - 1 : SPAN]
            faded = split(keys_t[head // group] * jnp.exp(last - cum_row))
            gathered = product(faded, solved)
            maps = unit * jnp.exp(last) - gathered[:, :DK]
            map_ref[head] = beside(*split(maps))
            add_ref[head] = gathered[:, DK:]

    def one_round(span, carried):
        before = jnp.maximum(span - 1, 0)
        follow(before)
        solve(before)
        prepare(span)
        return carried

    lax.fori_loop(0, spans, one_round, 0)
    follow(spans - 1)
    solve(spans - 1)
    for head in range(heads):
        fin_ref[head] = advance(head)
    turn = turn_ref[0]
    for place, end_ref in enumerate((end0, end1, end2, end3)):
        end_ref[...] = fin_ref[lax.rem(turn + place, heads)]


def query_kernel(
    query_ref, halo_ref, taps_ref, keyt_ref, solved_ref, start_ref, row_ref, col_ref, *rest
):
    local_out, carry_out, begin, finish = rest[-4:]
    width = query_ref.shape[1]
    key_heads = width // DK
    heads = solved_ref.shape[1]
    group = heads // key_heads
    halo = halo_ref[:, :width]

    def one_span(span, carried):
        here = pl.ds(span * SPAN, SPAN)
        ahead = pl.ds(max(span * SPAN - 16, 0), 16)
        feat = conv_silu(halo, query_ref[ahead, :], query_ref[here, :], taps_ref[...], span == 0)
        cum_rows = row_ref[:, here]
        cols = col_ref[here, :]
        queries, grams = [], []
        for key_head in range(key_heads):
            query = feat[:, key_head * DK : (key_head + 1) * DK]
            queries.append(query)
            grams.append(product(split(query), (keyt_ref[span, key_head, 0], keyt_ref[span, key_head, 1])))
        lifted = []
        for head in range(heads):
            gram = grams[head // group]
            top, low, end = decay_blocks(cols[:, head : head + 1], cum_rows[head : head + 1], False)
            high, fine = solved_ref[span, head, 0], solved_ref[span, head, 1]
            upper = product(split(gram[:HALF, :HALF] * top), (high[:HALF], fine[:HALF]))
            wide = beside(gram[HALF:, :HALF] * low, gram[HALF:, HALF:] * end)
            lifted.append(above(upper, product(split(wide), (high, fine))))
        for head in range(heads):
            exp_col = cols[:, 2 * heads + head : 2 * heads + head + 1]
            reach = queries[head // group] * exp_col - lifted[head][:, :DK]
            seen = product(split(reach), (start_ref[span, head, 0], start_ref[span, head, 1]))
            local_out[here, head * DV : (head + 1) * DV] = seen[:, :DV] + lifted[head][:, DK:]
            carry_out[here, head * 2 * DK : (head + 1) * 2 * DK] = beside(*split(seen[:, DV:]))
        return carried

    for span in range(begin, finish):
        one_span(span, 0)


def pack_kernel(query_ref, key_ref, val_ref, out_ref):
    out_ref[...] = beside(query_ref[...], key_ref[...], val_ref[...])


def compose_kernel(turn_ref, part0, part1, part2, part3, total_out, tail_out, prefix_out, all_ref):
    count = all_ref.shape[0]
    turn = turn_ref[0]
    for place, part in enumerate((part0, part1, part2, part3)):
        all_ref[lax.rem(turn + count - place, count)] = part[...]
    running = all_ref[0]
    prefix_out[0] = running
    for member in range(1, count):
        own = all_ref[member]
        moved = product(split(own[:, DV:]), split(running))
        running = beside(moved[:, :DV] + own[:, :DV], moved[:, DV:])
        if member < count - 1:
            prefix_out[member] = running
    total_out[...] = running
    tail_out[...] = running[:, :DV]


def enter_kernel(turn_ref, place_ref, near_ref, next_ref, far_ref, prefix_ref, out0, out1, out2, out3, all_ref):
    count = all_ref.shape[0]
    turn = turn_ref[0]
    place = place_ref[0]
    near, following, far = (
        jnp.where(place >= back, ref[...], 0.0)
        for back, ref in ((1, near_ref), (2, next_ref), (3, far_ref))
    )
    far = following[:, :DV] + product_small(split(following[:, DV:]), split(far))
    entry = near[:, :DV] + product_small(split(near[:, DV:]), split(far))
    parts = split(entry)
    all_ref[0] = entry
    for member in range(1, count):
        prefix = prefix_ref[member - 1]
        all_ref[member] = prefix[:, :DV] + product_small(split(prefix[:, DV:]), parts)
    for place, out in enumerate((out0, out1, out2, out3)):
        out[...] = all_ref[lax.rem(turn + place, count)]


def close_kernel(
    turn_ref, part0, part1, part2, part3, local_ref, carry_ref, gain_ref, out_ref, state_ref, done_ref, sems
):
    heads = state_ref.shape[0]
    turn = turn_ref[0]
    for place, part in enumerate((part0, part1, part2, part3)):
        pair = beside(*split(part[...]))
        state_ref[lax.rem(turn + heads - place, heads)] = above(pair, pair)
    spans = local_ref.shape[0] // SPAN

    def copy_out(span):
        here = pl.ds(span * SPAN, SPAN)
        return pltpu.make_async_copy(done_ref.at[here, :], out_ref.at[here, :], sems.at[span])

    def one_span(span, carried):
        here = pl.ds(span * SPAN, SPAN)
        for head in range(heads):
            both = dot(carry_ref[here, head * 2 * DK : (head + 1) * 2 * DK], state_ref[head])
            value = local_ref[here, head * DV : (head + 1) * DV] + both[:, :DV] + both[:, DV:]
            scale = lax.rsqrt(jnp.sum(value * value, axis=1, keepdims=True) * (1.0 / DV) + 1e-6)
            gain = gain_ref[:, head * DV : (head + 1) * DV]
            done_ref[here, head * DV : (head + 1) * DV] = (value * scale * gain).astype(bf16)
        copy_out(span).start()
        return carried

    def finish(span, carried):
        copy_out(span).wait()
        return carried

    for span in range(spans):
        one_span(span, 0)
    for span in range(spans):
        finish(span, 0)


def whole(shape):
    return pl.BlockSpec(shape, lambda *_: (0,) * len(shape))


def params(mebibytes):
    return pltpu.CompilerParams(dimension_semantics=("arbitrary",), vmem_limit_bytes=mebibytes * MIB)


def cost(flops, size, exps=0):
    return pl.CostEstimate(flops=flops, bytes_accessed=size, transcendentals=exps)


def per_device(
    query_in, key_in, value_in, log_decay, beta_gate, conv_query, conv_key, conv_value, norm_gain
):
    tok_rows, query_width = query_in.shape
    value_width = value_in.shape[1]
    key_heads = query_width // DK
    heads = value_width // DV
    spans = tok_rows // SPAN
    turn = lax.axis_index("outer").astype(jnp.int32).reshape(1)
    place = lax.axis_index("inner").astype(jnp.int32).reshape(1)
    far_in = tuple(
        pltpu.with_memory_space_constraint(array, pltpu.HBM) for array in (query_in, key_in, value_in)
    )
    tail_block = tok_rows // 16 - 1
    all_width = 2 * query_width + value_width
    tails = pl.pallas_call(
        pack_kernel,
        grid=(1,),
        in_specs=[
            pl.BlockSpec((16, query_width), lambda i: (tail_block, 0)),
            pl.BlockSpec((16, query_width), lambda i: (tail_block, 0)),
            pl.BlockSpec((16, value_width), lambda i: (tail_block, 0)),
        ],
        out_specs=whole((16, all_width)),
        out_shape=jax.ShapeDtypeStruct((16, all_width), bf16),
        compiler_params=params(4),
        cost_estimate=cost(0, 64_000),
        name="pack",
    )(*far_in)
    before = shifted(tails, ("inner", "outer"), 1, False)
    gates = above(log_decay.T, beta_gate.T)

    square = jax.ShapeDtypeStruct((DK, 2 * DV), f32)
    keyt, solved, starts, rows, cols, *ends = pl.pallas_call(
        state_kernel,
        grid_spec=pltpu.PrefetchScalarGridSpec(
            num_scalar_prefetch=1,
            grid=(),
            in_specs=[pl.BlockSpec(memory_space=pltpu.VMEM)] * 6,
            out_specs=[pl.BlockSpec(memory_space=pltpu.VMEM)] * 9,
            scratch_shapes=[
                pltpu.VMEM((heads, 2, DK, 2 * DV), bf16),
                pltpu.VMEM((heads, DK, 2 * DK), bf16),
                pltpu.VMEM((heads, DK, DV), f32),
                pltpu.VMEM((heads, DK, 2 * DV), f32),
                pltpu.VMEM((3, HALF, HALF), bf16),
                pltpu.VMEM((2 * HALF, (BASE - 1) * HALF), bf16),
                pltpu.VMEM((SPAN, SPAN), bf16),
                pltpu.VMEM((2 * heads, 2, HALF, HALF), bf16),
                pltpu.VMEM((heads, 2, HALF, HALF), bf16),
                pltpu.VMEM((key_heads, SPAN, DK), f32),
                pltpu.VMEM((key_heads, DK, SPAN), f32),
                pltpu.VMEM((SPAN, value_width), f32),
                pltpu.VMEM((SPAN, HALF), f32),
                pltpu.VMEM((2 * heads, SPAN), f32),
            ],
        ),
        out_shape=[
            jax.ShapeDtypeStruct((spans, key_heads, 2, DK, SPAN), bf16),
            jax.ShapeDtypeStruct((spans, heads, 2, SPAN, 2 * DV), bf16),
            jax.ShapeDtypeStruct((spans, heads, 2, DK, 2 * DV), bf16),
            jax.ShapeDtypeStruct((2 * heads, tok_rows), f32),
            jax.ShapeDtypeStruct((tok_rows, HALF), f32),
        ]
        + [square] * 4,
        compiler_params=pltpu.CompilerParams(vmem_limit_bytes=STATE_MIB * MIB),
        cost_estimate=cost(20_000_000_000, 20_000_000),
        name="state_path",
    )(turn, before, key_in, value_in, gates, conv_key, conv_value)

    parts = [ends[0]] + [shifted(ends[k], "outer", k, True) for k in (1, 2, 3)]

    out_types = (
        jax.ShapeDtypeStruct((tok_rows, value_width), f32),
        jax.ShapeDtypeStruct((tok_rows, 2 * value_width), bf16),
    )

    def query_part(offset, count, earlier):
        def body(*refs):
            query_kernel(*refs, offset, offset + count)

        return pl.pallas_call(
            body,
            in_specs=[pl.BlockSpec(memory_space=pltpu.VMEM)] * (8 + len(earlier)),
            out_specs=[pl.BlockSpec(memory_space=pltpu.VMEM)] * 2,
            out_shape=out_types,
            input_output_aliases={8 + k: k for k in range(len(earlier))},
            compiler_params=pltpu.CompilerParams(vmem_limit_bytes=QUERY_MIB * MIB),
            cost_estimate=cost(2_000_000_000 * count, 3_000_000 * count),
            name="query_path",
        )(query_in, before, conv_query, keyt, solved, starts, rows, cols, *earlier)

    cuts = (0, (3 * spans) // 8, (5 * spans) // 8, spans)
    seen = query_part(cuts[0], cuts[1] - cuts[0], ())
    parts, seen = lax.optimization_barrier((parts, seen))

    total, tail, prefix = pl.pallas_call(
        compose_kernel,
        grid_spec=pltpu.PrefetchScalarGridSpec(
            num_scalar_prefetch=1,
            grid=(1,),
            in_specs=[whole((DK, 2 * DV))] * 4,
            out_specs=[whole((DK, 2 * DV)), whole((DK, DV)), whole((3, DK, 2 * DV))],
            scratch_shapes=[pltpu.VMEM((4, DK, 2 * DV), f32)],
        ),
        out_shape=[
            square,
            jax.ShapeDtypeStruct((DK, DV), f32),
            jax.ShapeDtypeStruct((3, DK, 2 * DV), f32),
        ],
        compiler_params=params(8),
        cost_estimate=cost(100_000_000, 1_000_000),
        name="compose",
    )(turn, *parts)
    near = shifted(total, "inner", 1, True)
    middle = shifted(total, "inner", 2, True)
    far = shifted(tail, "inner", 3, True)

    seen = query_part(cuts[1], cuts[2] - cuts[1], seen)
    near, seen = lax.optimization_barrier((near, seen))
    local, carry = query_part(cuts[2], cuts[3] - cuts[2], seen)

    entries = pl.pallas_call(
        enter_kernel,
        grid_spec=pltpu.PrefetchScalarGridSpec(
            num_scalar_prefetch=2,
            grid=(1,),
            in_specs=[whole((DK, 2 * DV)), whole((DK, 2 * DV)), whole((DK, DV)), whole((3, DK, 2 * DV))],
            out_specs=[whole((DK, DV))] * 4,
            scratch_shapes=[pltpu.VMEM((4, DK, DV), f32)],
        ),
        out_shape=[jax.ShapeDtypeStruct((DK, DV), f32)] * 4,
        compiler_params=params(8),
        cost_estimate=cost(50_000_000, 1_000_000),
        name="enter",
    )(turn, place, near, middle, far, prefix)
    states = [entries[0]] + [shifted(entries[k], "outer", k, True) for k in (1, 2, 3)]

    return pl.pallas_call(
        close_kernel,
        grid_spec=pltpu.PrefetchScalarGridSpec(
            num_scalar_prefetch=1,
            grid=(),
            in_specs=[pl.BlockSpec(memory_space=pltpu.VMEM)] * 7,
            out_specs=pl.BlockSpec(memory_space=pltpu.HBM),
            scratch_shapes=[
                pltpu.VMEM((heads, 2 * DK, 2 * DV), bf16),
                pltpu.VMEM((tok_rows, value_width), bf16),
                pltpu.SemaphoreType.DMA((spans,)),
            ],
        ),
        out_shape=jax.ShapeDtypeStruct((tok_rows, value_width), bf16),
        compiler_params=pltpu.CompilerParams(vmem_limit_bytes=12 * MIB),
        cost_estimate=cost(2_000_000_000, 10_000_000),
        name="close",
    )(turn, *states, local, carry, norm_gain.reshape(1, value_width))


def solution(mesh):
    in_specs = (
        P(("inner", "outer"), "head"),
        P(("inner", "outer"), "head"),
        P(("inner", "outer"), "head"),
        P(("inner", "outer"), "head"),
        P(("inner", "outer"), "head"),
        P(None, "head"),
        P(None, "head"),
        P(None, "head"),
        P("head"),
    )
    out_specs = P(("inner", "outer"), "head")
    return jax.shard_map(
        per_device, mesh=mesh, in_specs=in_specs, out_specs=out_specs, check_vma=False
    )
```

time: 70.4 us -> 67.7 us (0.962)
  Pallas kernels: 44.6 us -> 41 us
    pallas_call x1, Pallas kernels: 4.88 us -> 2.74 us  [per_device(): pl.pallas_call(close_kernel, grid_spec=pltpu.PrefetchScalarGridSpec(num_s...]
    pallas_call x3, Pallas kernels: 9.5 us -> 8.3 us  [query_part(): pl.pallas_call(body, in_specs=[pl.BlockSpec(memory_space=pltpu.VMEM)] * (...]
  transfers between devices with their start and end apart: 10 -> 10, of which waited for: 3 -> 5; matrix products, arithmetic and copies ran while one was open for 0% -> 0% of each run, Pallas kernels for 14% -> 12%
where the time goes in v3:
time: 67.7 us; the launch traced here: 67.5 us
  Pallas kernels  41 us (61%)
  starting transfers between devices  22.1 us (33%)
  waiting for transfers between devices  4.01 us (6%)
    pallas_call x1, Pallas kernels, per_device(): pl.pallas_call(state_kernel, grid_spec=pltpu.PrefetchScalarGridSpec(num_s...  27.8 us
    ppermute x10, starting transfers between devices, shifted(): return lax.ppermute(value, axis, pairs)  22.1 us
    pallas_call x3, Pallas kernels, query_part(): pl.pallas_call(body, in_specs=[pl.BlockSpec(memory_space=pltpu.VMEM)] * (...  8.3 us
    ppermute x10, waiting for transfers between devices, shifted(): return lax.ppermute(value, axis, pairs)  4.01 us
    pallas_call x1, Pallas kernels, per_device(): pl.pallas_call(close_kernel, grid_spec=pltpu.PrefetchScalarGridSpec(num_s...  2.74 us
  transfers between devices with their start and end apart: 10, of which 5 were waited for; matrix products, arithmetic and copies ran while one was open for 0% of the time, Pallas kernels for 12%

profile of v3, /device:TPU:0, one launch (start us, length us, event | category | flops | bytes accessed | tf_op | source)
XLA Modules:
  0.0 67.5 jit_solution(231453940335022433)
XLA Ops:
  0.0 0.9 %pack.1 = bf16[16,1024]{1,0:T(8,128)(2,1)S(1)} custom-call(bf16[2048,256]{1,0:T(8,128)(2,1)} %refs_0_.5, bf16[2048,256]{1,0:T(8,128)(2,1)} %key_ref.3, bf16[2048,512]{1,0:T(8,128)(2,1)} %val_ref.3), custom_call_target="tpu_custom_call" | custom-call | bytes 64000 | tf_op jit(solution)/shard_map/pack/pallas_call | solution.py:442
  0.9 3.7 %collective-permute-start = (bf16[16,1024]{1,0:T(8,128)(2,1)S(1)}, bf16[16,1024]{1,0:T(8,128)(2,1)S(1)}, u32[]{:S(2)}, u32[]{:S(2)}) collective-permute-start(bf16[16,1024]{1,0:T(8,128)(2,1)S(1)} %pack.1), channel_id=1, source_target_pairs={{0,1},{1,2},{2,3},{3,4},{4,5},{5,6},{6,7},{7,8},{8,9},{9,10},{10,1... | collective-permute-start | bytes 98312 | tf_op jit(solution)/shard_map/ppermute | solution.py:28
  4.6 0.0 copy-done.7
  4.6 0.0 copy-done.8
  4.7 1.5 %collective-permute-done.halo_ref.refs_1_ = bf16[16,1024]{1,0:T(8,128)(2,1)S(1)} collective-permute-done((bf16[16,1024]{1,0:T(8,128)(2,1)S(1)}, bf16[16,1024]{1,0:T(8,128)(2,1)S(1)}, u32[]{:S(2)}, u32[]{:S(2)}) %collective-permute-start) | collective-permute-done | bytes 32800 | tf_op jit(solution)/shard_map/ppermute | solution.py:28
  6.2 0.0 copy-start
  6.2 0.0 copy-start.3
  6.3 27.8 %state_path.1 = (bf16[8,2,2,128,256]{4,3,2,1,0:T(8,128)(2,1)S(1)}, bf16[8,4,2,256,256]{4,3,2,1,0:T(8,128)(2,1)S(1)}, bf16[8,4,2,128,256]{4,3,2,1,0:T(8,128)(2,1)...) custom-call(s32[1]{0:T(128)} %bitcast.turn_ref, ...), custom_call_target="tpu_custom_call" | custom-call | flops 20000000000 | bytes 20000000 | tf_op jit(solution)/shard_map/state_path/pallas_call | solution.py:460
  34.1 2.4 %collective-permute-start.1 = (f32[128,256]{1,0:T(8,128)S(1)}, f32[128,256]{1,0:T(8,128)S(1)}, u32[]{:S(2)}, u32[]{:S(2)}) collective-permute-start(f32[128,256]{1,0:T(8,128)S(1)} %get-tuple-element.37), channel_id=1, source_target_pairs={{0,1},{1,2},{2,3},{3,0},{4,5},{5,6},{6,7},{7,4},{8,9},{9,10},{10,1... | collective-permute-start | bytes 393224 | tf_op jit(solution)/shard_map/ppermute | solution.py:28
  36.5 2.9 %collective-permute-start.2 = (f32[128,256]{1,0:T(8,128)S(1)}, f32[128,256]{1,0:T(8,128)S(1)}, u32[]{:S(2)}, u32[]{:S(2)}) collective-permute-start(f32[128,256]{1,0:T(8,128)S(1)} %get-tuple-element.38), channel_id=1, source_target_pairs={{0,2},{1,3},{2,0},{3,1},{4,6},{5,7},{6,4},{7,5},{8,10},{9,11},{10,... | collective-permute-start | bytes 393224 | tf_op jit(solution)/shard_map/ppermute | solution.py:28
  39.4 1.3 %collective-permute-start.3 = (f32[128,256]{1,0:T(8,128)S(1)}, f32[128,256]{1,0:T(8,128)S(1)}, u32[]{:S(2)}, u32[]{:S(2)}) collective-permute-start(f32[128,256]{1,0:T(8,128)S(1)} %get-tuple-element.39), channel_id=1, source_target_pairs={{0,3},{1,0},{2,1},{3,2},{4,7},{5,4},{6,5},{7,6},{8,11},{9,8},{10,9... | collective-permute-start | bytes 393224 | tf_op jit(solution)/shard_map/ppermute | solution.py:28
  40.7 3.1 %query_path.3 = (f32[2048,512]{1,0:T(8,128)S(1)}, bf16[2048,1024]{1,0:T(8,128)(2,1)S(1)}) custom-call(bf16[2048,256]{1,0:T(8,128)(2,1)S(1)} %copy-done, bf16[16,1024]{1,0:T(8,128)(2,1)S(1)} %collective-permute-done.halo_ref.refs_1_, bf16[4,256]{1,0:T(4,128)(2,1)S(1)} %copy-done.3, bf16[8,2,2,128,256]{4,3,2,1,0:T(8,128)(2,1)S(1)} %get-tuple-element.40.refs_3_, ...), custom_call_target="tpu_custom_call" | custom-call | flops 6000000000 | bytes 9000000 | tf_op jit(solution)/shard_map/query_path/pallas_call | solution.py:508
  43.8 0.0 collective-permute-done.1.part1
  43.9 0.4 collective-permute-done.2.part2
  44.3 0.1 collective-permute-done.3.part3
  44.4 0.6 compose.1
  45.0 4.5 %collective-permute-start.5 = (f32[128,256]{1,0:T(8,128)S(1)}, f32[128,256]{1,0:T(8,128)S(1)}, u32[]{:S(2)}, u32[]{:S(2)}) collective-permute-start(f32[128,256]{1,0:T(8,128)S(1)} %get-tuple-element.51), channel_id=1, source_target_pairs={{0,8},{4,12},{8,0},{12,4},{1,9},{5,13},{9,1},{13,5},{2,10},{6,14},... | collective-permute-start | bytes 393224 | tf_op jit(solution)/shard_map/ppermute | solution.py:28
  49.5 0.6 collective-permute-start.4
  50.1 2.7 %collective-permute-start.6 = (f32[128,128]{1,0:T(8,128)S(1)}, f32[128,128]{1,0:T(8,128)S(1)}, u32[]{:S(2)}, u32[]{:S(2)}) collective-permute-start(f32[128,128]{1,0:T(8,128)S(1)} %get-tuple-element.57), channel_id=1, source_target_pairs={{0,12},{4,0},{8,4},{12,8},{1,13},{5,1},{9,5},{13,9},{2,14},{6,2},{... | collective-permute-start | bytes 196616 | tf_op jit(solution)/shard_map/ppermute | solution.py:28
  52.8 2.1 %query_path.4 = (f32[2048,512]{1,0:T(8,128)S(1)}, bf16[2048,1024]{1,0:T(8,128)(2,1)S(1)}) custom-call(bf16[2048,256]{1,0:T(8,128)(2,1)S(1)} %copy-done, bf16[16,1024]{1,0:T(8,128)(2,1)S(1)} %collective-permute-done.halo_ref.refs_1_, bf16[4,256]{1,0:T(4,128)(2,1)S(1)} %copy-done.3, ...), custom_call_target="tpu_custom_call", output_to_operand_aliasing={{0}: (8, {}), {1}: (9, {})} | custom-call | flops 4000000000 | bytes 6000000 | tf_op jit(solution)/shard_map/query_path/pallas_call | solution.py:508
  54.9 0.8 %collective-permute-done.4.near_ref = f32[128,256]{1,0:T(8,128)S(1)} collective-permute-done((f32[128,256]{1,0:T(8,128)S(1)}, f32[128,256]{1,0:T(8,128)S(1)}, u32[]{:S(2)}, u32[]{:S(2)}) %collective-permute-start.4) | collective-permute-done | bytes 131104 | tf_op jit(solution)/shard_map/ppermute | solution.py:28
  55.7 0.0 collective-permute-done.6.far_ref
  55.7 0.0 collective-permute-done.5.next_ref
  55.7 0.6 enter.1
  56.3 0.5 collective-permute-start.7
  56.8 3.6 %collective-permute-start.8 = (f32[128,128]{1,0:T(8,128)S(1)}, f32[128,128]{1,0:T(8,128)S(1)}, u32[]{:S(2)}, u32[]{:S(2)}) collective-permute-start(f32[128,128]{1,0:T(8,128)S(1)} %get-tuple-element.61), channel_id=1, source_target_pairs={{0,2},{1,3},{2,0},{3,1},{4,6},{5,7},{6,4},{7,5},{8,10},{9,11},{10,... | collective-permute-start | bytes 196616 | tf_op jit(solution)/shard_map/ppermute | solution.py:28
  60.4 0.0 collective-permute-start.9
  60.4 3.1 %query_path.5 = (f32[2048,512]{1,0:T(8,128)S(1)}, bf16[2048,1024]{1,0:T(8,128)(2,1)S(1)}) custom-call(bf16[2048,256]{1,0:T(8,128)(2,1)S(1)} %copy-done, bf16[16,1024]{1,0:T(8,128)(2,1)S(1)} %collective-permute-done.halo_ref.refs_1_, bf16[4,256]{1,0:T(4,128)(2,1)S(1)} %copy-done.3, ...), custom_call_target="tpu_custom_call", output_to_operand_aliasing={{0}: (8, {}), {1}: (9, {})} | custom-call | flops 6000000000 | bytes 9000000 | tf_op jit(solution)/shard_map/query_path/pallas_call | solution.py:508
  63.4 0.0 collective-permute-done.7.part1
  63.5 0.0 collective-permute-done.8.part2
  63.5 1.1 %collective-permute-done.9.part3 = f32[128,128]{1,0:T(8,128)S(1)} collective-permute-done((f32[128,128]{1,0:T(8,128)S(1)}, f32[128,128]{1,0:T(8,128)S(1)}, u32[]{:S(2)}, u32[]{:S(2)}) %collective-permute-start.9) | collective-permute-done | bytes 65568 | tf_op jit(solution)/shard_map/ppermute | solution.py:28
  64.6 2.7 %close.1 = bf16[2048,512]{1,0:T(8,128)(2,1)} custom-call(s32[1]{0:T(128)} %bitcast.turn_ref, f32[128,128]{1,0:T(8,128)S(1)} %get-tuple-element.59.part0, f32[128,128]{1,0:T(8,128)S(1)} %collective-permute-done.7.part1, f32[128,128]{1,0:T(8,128)S(1)} %collective-permute-done.8.part2, f32[128,128]{1,0:T(8,128)S(1)} %collective-permute-done.9.part3, ...), custom_call_target="tpu_custom_call" | custom-call | flops 2000000000 | bytes 10000000 | tf_op jit(solution)/shard_map/close/pallas_call | solution.py:565
  (15 shorter events, 0.0 us)
Async XLA Ops:
  0.0 6.2 %copy-start.1 = (bf16[2048,512]{1,0:T(8,128)(2,1)S(1)}, bf16[2048,512]{1,0:T(8,128)(2,1)}, u32[]{:S(2)}) copy-start(bf16[2048,512]{1,0:T(8,128)(2,1)} %val_ref.3) | copy-start | bytes 6291460
  0.0 6.2 %copy-start.2 = (bf16[2048,256]{1,0:T(8,128)(2,1)S(1)}, bf16[2048,256]{1,0:T(8,128)(2,1)}, u32[]{:S(2)}) copy-start(bf16[2048,256]{1,0:T(8,128)(2,1)} %key_ref.3) | copy-start | bytes 3145732
  0.0 4.6 %copy-start.7 = (f32[2048,4]{0,1:T(4,128)S(1)}, f32[2048,4]{0,1:T(4,128)}, u32[]{:S(2)}) copy-start(f32[2048,4]{0,1:T(4,128)} %param.13) | copy-start | bytes 98308
  0.0 4.6 %copy-start.8 = (f32[2048,4]{0,1:T(4,128)S(1)}, f32[2048,4]{0,1:T(4,128)}, u32[]{:S(2)}) copy-start(f32[2048,4]{0,1:T(4,128)} %param.12) | copy-start | bytes 98308
  0.0 6.2 %copy-start.5 = (bf16[4,512]{1,0:T(4,128)(2,1)S(1)}, bf16[4,512]{1,0:T(4,128)(2,1)}, u32[]{:S(2)}) copy-start(bf16[4,512]{1,0:T(4,128)(2,1)} %val_taps.1) | copy-start | bytes 12292
  0.0 6.2 %copy-start.6 = (bf16[4,256]{1,0:T(4,128)(2,1)S(1)}, bf16[4,256]{1,0:T(4,128)(2,1)}, u32[]{:S(2)}) copy-start(bf16[4,256]{1,0:T(4,128)(2,1)} %key_taps.1) | copy-start | bytes 6148
  0.9 5.3 %collective-permute-start = (bf16[16,1024]{1,0:T(8,128)(2,1)S(1)}, bf16[16,1024]{1,0:T(8,128)(2,1)S(1)}, u32[]{:S(2)}, u32[]{:S(2)}) collective-permute-start(bf16[16,1024]{1,0:T(8,128)(2,1)S(1)} %pack.1), channel_id=1, source_target_pairs={{0,1},{1,2},{2,3},{3,4},{4,5},{5,6},{6,7},{7,8},{8,9},{9,10},{10,1... | collective-permute-start | bytes 98312 | tf_op jit(solution)/shard_map/ppermute | solution.py:28
  6.2 34.5 %copy-start = (bf16[2048,256]{1,0:T(8,128)(2,1)S(1)}, bf16[2048,256]{1,0:T(8,128)(2,1)}, u32[]{:S(2)}) copy-start(bf16[2048,256]{1,0:T(8,128)(2,1)} %refs_0_.5) | copy-start | bytes 3145732
  6.2 34.5 %copy-start.3 = (bf16[4,256]{1,0:T(4,128)(2,1)S(1)}, bf16[4,256]{1,0:T(4,128)(2,1)}, u32[]{:S(2)}) copy-start(bf16[4,256]{1,0:T(4,128)(2,1)} %refs_2_.5) | copy-start | bytes 6148
  34.1 9.7 %collective-permute-start.1 = (f32[128,256]{1,0:T(8,128)S(1)}, f32[128,256]{1,0:T(8,128)S(1)}, u32[]{:S(2)}, u32[]{:S(2)}) collective-permute-start(f32[128,256]{1,0:T(8,128)S(1)} %get-tuple-element.37), channel_id=1, source_target_pairs={{0,1},{1,2},{2,3},{3,0},{4,5},{5,6},{6,7},{7,4},{8,9},{9,10},{10,1... | collective-permute-start | bytes 393224 | tf_op jit(solution)/shard_map/ppermute | solution.py:28
  36.5 7.8 %collective-permute-start.2 = (f32[128,256]{1,0:T(8,128)S(1)}, f32[128,256]{1,0:T(8,128)S(1)}, u32[]{:S(2)}, u32[]{:S(2)}) collective-permute-start(f32[128,256]{1,0:T(8,128)S(1)} %get-tuple-element.38), channel_id=1, source_target_pairs={{0,2},{1,3},{2,0},{3,1},{4,6},{5,7},{6,4},{7,5},{8,10},{9,11},{10,... | collective-permute-start | bytes 393224 | tf_op jit(solution)/shard_map/ppermute | solution.py:28
  39.4 5.0 %collective-permute-start.3 = (f32[128,256]{1,0:T(8,128)S(1)}, f32[128,256]{1,0:T(8,128)S(1)}, u32[]{:S(2)}, u32[]{:S(2)}) collective-permute-start(f32[128,256]{1,0:T(8,128)S(1)} %get-tuple-element.39), channel_id=1, source_target_pairs={{0,3},{1,0},{2,1},{3,2},{4,7},{5,4},{6,5},{7,6},{8,11},{9,8},{10,9... | collective-permute-start | bytes 393224 | tf_op jit(solution)/shard_map/ppermute | solution.py:28
  45.0 10.7 %collective-permute-start.5 = (f32[128,256]{1,0:T(8,128)S(1)}, f32[128,256]{1,0:T(8,128)S(1)}, u32[]{:S(2)}, u32[]{:S(2)}) collective-permute-start(f32[128,256]{1,0:T(8,128)S(1)} %get-tuple-element.51), channel_id=1, source_target_pairs={{0,8},{4,12},{8,0},{12,4},{1,9},{5,13},{9,1},{13,5},{2,10},{6,14},... | collective-permute-start | bytes 393224 | tf_op jit(solution)/shard_map/ppermute | solution.py:28
  49.5 6.2 %collective-permute-start.4 = (f32[128,256]{1,0:T(8,128)S(1)}, f32[128,256]{1,0:T(8,128)S(1)}, u32[]{:S(2)}, u32[]{:S(2)}) collective-permute-start(f32[128,256]{1,0:T(8,128)S(1)} %get-tuple-element.51), channel_id=1, source_target_pairs={{0,4},{4,8},{8,12},{12,0},{1,5},{5,9},{9,13},{13,1},{2,6},{6,10},{... | collective-permute-start | bytes 393224 | tf_op jit(solution)/shard_map/ppermute | solution.py:28
  50.1 5.6 %collective-permute-start.6 = (f32[128,128]{1,0:T(8,128)S(1)}, f32[128,128]{1,0:T(8,128)S(1)}, u32[]{:S(2)}, u32[]{:S(2)}) collective-permute-start(f32[128,128]{1,0:T(8,128)S(1)} %get-tuple-element.57), channel_id=1, source_target_pairs={{0,12},{4,0},{8,4},{12,8},{1,13},{5,1},{9,5},{13,9},{2,14},{6,2},{... | collective-permute-start | bytes 196616 | tf_op jit(solution)/shard_map/ppermute | solution.py:28
  56.3 7.1 %collective-permute-start.7 = (f32[128,128]{1,0:T(8,128)S(1)}, f32[128,128]{1,0:T(8,128)S(1)}, u32[]{:S(2)}, u32[]{:S(2)}) collective-permute-start(f32[128,128]{1,0:T(8,128)S(1)} %get-tuple-element.60), channel_id=1, source_target_pairs={{0,1},{1,2},{2,3},{3,0},{4,5},{5,6},{6,7},{7,4},{8,9},{9,10},{10,1... | collective-permute-start | bytes 196616 | tf_op jit(solution)/shard_map/ppermute | solution.py:28
  56.8 6.7 %collective-permute-start.8 = (f32[128,128]{1,0:T(8,128)S(1)}, f32[128,128]{1,0:T(8,128)S(1)}, u32[]{:S(2)}, u32[]{:S(2)}) collective-permute-start(f32[128,128]{1,0:T(8,128)S(1)} %get-tuple-element.61), channel_id=1, source_target_pairs={{0,2},{1,3},{2,0},{3,1},{4,6},{5,7},{6,4},{7,5},{8,10},{9,11},{10,... | collective-permute-start | bytes 196616 | tf_op jit(solution)/shard_map/ppermute | solution.py:28
  60.3 4.3 %copy-start.4 = (f32[512]{0:T(512)S(1)}, f32[512]{0:T(512)}, u32[]{:S(2)}) copy-start(f32[512]{0:T(512)} %param.17) | copy-start | bytes 6148
  60.4 4.3 %collective-permute-start.9 = (f32[128,128]{1,0:T(8,128)S(1)}, f32[128,128]{1,0:T(8,128)S(1)}, u32[]{:S(2)}, u32[]{:S(2)}) collective-permute-start(f32[128,128]{1,0:T(8,128)S(1)} %get-tuple-element.62), channel_id=1, source_target_pairs={{0,3},{1,0},{2,1},{3,2},{4,7},{5,4},{6,5},{7,6},{8,11},{9,8},{10,9... | collective-permute-start | bytes 196616 | tf_op jit(solution)/shard_map/ppermute | solution.py:28

commit v4 on v3

--- a/solution.py
+++ b/solution.py
@@ -11,8 +11,9 @@
 SPAN = 256
 HALF = 128
 BASE = 16
+GROUP = 2
 MIB = 1024 * 1024
-STATE_MIB = 16
+STATE_MIB = 24
 QUERY_MIB = 14
 
 f32 = jnp.float32
@@ -120,8 +121,9 @@
     for head in range(heads):
         run_ref[head, 0] = beside(zeros, unit).astype(bf16)
         run_ref[head, 1] = beside(zeros, zeros).astype(bf16)
-        map_ref[head] = beside(unit, zeros).astype(bf16)
-        add_ref[head] = zeros
+        for sub in range(GROUP):
+            map_ref[sub, head] = beside(unit, zeros).astype(bf16)
+            add_ref[sub, head] = zeros
     size = BASE
     for level in range(level_ref.shape[0]):
         picked = (
@@ -136,70 +138,77 @@
         pick_ref[:, place * HALF : (place + 1) * HALF] = above(chosen, chosen)
     tri_rows, tri_cols = iotas((SPAN, SPAN))
     tri_ref[...] = jnp.where(tri_rows <= tri_cols, 1.0, 0.0).astype(bf16)
-    for ref in (inv_ref, below_ref, keyed_ref, turned_ref, feat_ref, held_ref, cum_ref):
-        ref[...] = jnp.zeros(ref.shape, ref.dtype)
-
-    def advance(head):
-        maps = map_ref[head]
-        high, low = run_ref[head, 0], run_ref[head, 1]
+
+    def advance(head, sub, high, low):
+        maps = map_ref[sub, head]
         moved = dot(maps, above(high, high)) + dot(maps[:, :DK], low)
-        return beside(moved[:, :DV] + add_ref[head], moved[:, DV:])
-
-    def follow(span):
+        return beside(moved[:, :DV] + add_ref[sub, head], moved[:, DV:])
+
+    def follow(group_at):
         for head in range(heads):
-            high, low = split(advance(head))
+            high, low = run_ref[head, 0], run_ref[head, 1]
+            for sub in range(GROUP):
+                start_out[group_at * GROUP + sub, head, 0] = high
+                start_out[group_at * GROUP + sub, head, 1] = low
+                reached = advance(head, sub, high, low)
+                high, low = split(reached)
             run_ref[head, 0] = high
             run_ref[head, 1] = low
-            start_out[span, head, 0] = high
-            start_out[span, head, 1] = low
-
-    def prepare(span):
-        rows_at = pl.multiple_of(span * SPAN, SPAN)
-        here = pl.ds(rows_at, SPAN)
-        ahead = pl.ds(pl.multiple_of(jnp.maximum(rows_at - 16, 0), 16), 16)
-        gates = gate_ref[:, here]
-        is_log = lax.broadcasted_iota(jnp.int32, gates.shape, 0) < heads
-        logs = jnp.where(is_log, gates, 0.0)
-        logs = above(logs, logs)
-        high = logs.astype(bf16)
-        rest = logs - high.astype(f32)
-        mid = rest.astype(bf16)
-        low = (rest - mid.astype(f32)).astype(bf16)
-        tri = tri_ref[...]
-        cum = (dot(high, tri) + dot(mid, tri) + dot(low, tri))[: gates.shape[0]]
-        row_out[:, here] = cum
-        packed = above(
-            jnp.where(is_log, cum, gates),
-            jnp.exp(cum),
-            jnp.zeros((HALF - 2 * gates.shape[0], SPAN), f32),
-        )
-        cols = packed.T
-        col_out[here, :] = cols
-
-        first = span == 0
-        key_feat = conv_silu(halo[:, width : 2 * width], key_ref[ahead, :], key_ref[here, :], key_taps[...], first)
-        val_feat = conv_silu(halo[:, 2 * width :], val_ref[ahead, :], val_ref[here, :], val_taps[...], first)
-
-        keys, keys_t, grams = [], [], []
-        for key_head in range(key_heads):
-            feat = key_feat[:, key_head * DK : (key_head + 1) * DK]
-            keyed = feat * lax.rsqrt(jnp.sum(feat * feat, axis=1, keepdims=True) + 1e-6)
-            turned = keyed.T
-            parts = split(turned)
-            keyt_out[span, key_head, 0] = parts[0]
-            keyt_out[span, key_head, 1] = parts[1]
-            keys.append(keyed)
-            keys_t.append(turned)
-            grams.append(product(split(keyed), parts))
-
-        diag, below = [], []
-        for head in range(heads):
-            gram = grams[head // group]
-            beta_col = cols[:, heads + head : heads + head + 1]
-            top, low, end = decay_blocks(cols[:, head : head + 1], cum[head : head + 1], True)
-            diag.append(gram[:HALF, :HALF] * top * beta_col[:HALF])
-            below.append(split(gram[HALF:, :HALF] * low * beta_col[HALF:]))
-            diag.append(gram[HALF:, HALF:] * end * beta_col[HALF:])
+            fin_ref[head] = reached
+
+    def prepare(group_at):
+        feats = []
+        for sub in range(GROUP):
+            span = group_at * GROUP + sub
+            rows_at = pl.multiple_of(span * SPAN, SPAN)
+            here = pl.ds(rows_at, SPAN)
+            ahead = pl.ds(pl.multiple_of(jnp.maximum(rows_at - 16, 0), 16), 16)
+            gates = gate_ref[:, here]
+            is_log = lax.broadcasted_iota(jnp.int32, gates.shape, 0) < heads
+            logs = jnp.where(is_log, gates, 0.0)
+            logs = above(logs, logs)
+            high = logs.astype(bf16)
+            rest = logs - high.astype(f32)
+            mid = rest.astype(bf16)
+            low = (rest - mid.astype(f32)).astype(bf16)
+            tri = tri_ref[...]
+            cum = (dot(high, tri) + dot(mid, tri) + dot(low, tri))[: gates.shape[0]]
+            row_out[:, here] = cum
+            packed = above(
+                jnp.where(is_log, cum, gates),
+                jnp.exp(cum),
+                jnp.zeros((HALF - 2 * gates.shape[0], SPAN), f32),
+            )
+            cols = packed.T
+            col_out[here, :] = cols
+            first = span == 0
+            key_feat = conv_silu(
+                halo[:, width : 2 * width], key_ref[ahead, :], key_ref[here, :], key_taps[...], first
+            )
+            val_feat = conv_silu(
+                halo[:, 2 * width :], val_ref[ahead, :], val_ref[here, :], val_taps[...], first
+            )
+            feats.append((span, cum, cols, key_feat, val_feat))
+
+        diag, below, keyed_all = [], [], []
+        for span, cum, cols, key_feat, _ in feats:
+            grams = []
+            for key_head in range(key_heads):
+                feat = key_feat[:, key_head * DK : (key_head + 1) * DK]
+                keyed = feat * lax.rsqrt(jnp.sum(feat * feat, axis=1, keepdims=True) + 1e-6)
+                turned = keyed.T
+                parts = split(turned)
+                keyt_out[span, key_head, 0] = parts[0]
+                keyt_out[span, key_head, 1] = parts[1]
+                keyed_all.append((keyed, turned))
+                grams.append(product(split(keyed), parts))
+            for head in range(heads):
+                gram = grams[head // group]
+                beta_col = cols[:, heads + head : heads + head + 1]
+                top, low, end = decay_blocks(cols[:, head : head + 1], cum[head : head + 1], True)
+                diag.append(gram[:HALF, :HALF] * top * beta_col[:HALF])
+                below.append(split(gram[HALF:, :HALF] * low * beta_col[HALF:]))
+                diag.append(gram[HALF:, HALF:] * end * beta_col[HALF:])
 
         blocks = HALF // BASE
         compact = above(
@@ -214,7 +223,9 @@
             factor = spread[:, place * HALF : (place + 1) * HALF].reshape(count, BASE, HALF)
             small = small - factor * small[:, place : place + 1, :]
         inverses = [
-            jnp.where(base_mask, jnp.broadcast_to(small[item][None], (blocks, BASE, HALF)).reshape(HALF, HALF), 0.0)
+            jnp.where(
+                base_mask, jnp.broadcast_to(small[item][None], (blocks, BASE, HALF)).reshape(HALF, HALF), 0.0
+            )
             for item in range(count)
         ]
         diag_parts = [split(item) for item in diag]
@@ -240,57 +251,60 @@
 
         for item in range(count):
             inv_ref[item, 0], inv_ref[item, 1] = inv_parts[item]
-        for head in range(heads):
-            below_ref[head, 0], below_ref[head, 1] = below[head]
-        for key_head in range(key_heads):
-            keyed_ref[key_head] = keys[key_head]
-            turned_ref[key_head] = keys_t[key_head]
-        feat_ref[...] = val_feat
-        held_ref[...] = cols
-        cum_ref[...] = cum
-
-    def solve(span):
-        inv_parts = [(inv_ref[item, 0], inv_ref[item, 1]) for item in range(2 * heads)]
-        below = [(below_ref[head, 0], below_ref[head, 1]) for head in range(heads)]
-        keys = [keyed_ref[key_head] for key_head in range(key_heads)]
-        keys_t = [turned_ref[key_head] for key_head in range(key_heads)]
-        val_feat, cols, cum = feat_ref[...], held_ref[...], cum_ref[...]
-        right, tops, lows = [], [], []
-        for head in range(heads):
+        for item, parts in enumerate(below):
+            below_ref[item, 0], below_ref[item, 1] = parts
+        for item, (keyed, turned) in enumerate(keyed_all):
+            keyed_ref[item] = keyed
+            turned_ref[item] = turned
+        for sub, (_, cum, cols, _, val_feat) in enumerate(feats):
+            feat_ref[sub] = val_feat
+            held_ref[sub] = cols
+            cum_ref[sub] = cum
+
+    def solve(group_at):
+        both = [(sub, head) for sub in range(GROUP) for head in range(heads)]
+        tops, lows, right = [], [], []
+        for sub, head in both:
+            cols = held_ref[sub]
             beta_col = cols[:, heads + head : heads + head + 1]
             exp_col = cols[:, 2 * heads + head : 2 * heads + head + 1]
-            right.append(
-                beside(keys[head // group] * (beta_col * exp_col), val_feat[:, head * DV : (head + 1) * DV] * beta_col)
-            )
-        for head in range(heads):
-            tops.append(split(product(inv_parts[2 * head], split(right[head][:HALF]))))
-        for head in range(heads):
-            rest = right[head][HALF:] - product(below[head], tops[head])
-            lows.append(split(product(inv_parts[2 * head + 1], split(rest))))
-        for head in range(heads):
-            solved = (above(tops[head][0], lows[head][0]), above(tops[head][1], lows[head][1]))
-            solved_out[span, head, 0] = solved[0]
-            solved_out[span, head, 1] = solved[1]
-            cum_row = cum[head : head + 1]
+            keyed = keyed_ref[sub * key_heads + head // group]
+            value = feat_ref[sub, :, head * DV : (head + 1) * DV]
+            right.append(beside(keyed * (beta_col * exp_col), value * beta_col))
+        for sub, head in both:
+            item = sub * heads + head
+            inv = (inv_ref[2 * item, 0], inv_ref[2 * item, 1])
+            tops.append(split(product(inv, split(right[item][:HALF]))))
+        for sub, head in both:
+            item = sub * heads + head
+            rest = right[item][HALF:] - product((below_ref[item, 0], below_ref[item, 1]), tops[item])
+            inv = (inv_ref[2 * item + 1, 0], inv_ref[2 * item + 1, 1])
+            lows.append(split(product(inv, split(rest))))
+        for sub, head in both:
+            item = sub * heads + head
+            solved = (above(tops[item][0], lows[item][0]), above(tops[item][1], lows[item][1]))
+            solved_out[group_at * GROUP + sub, head, 0] = solved[0]
+            solved_out[group_at * GROUP + sub, head, 1] = solved[1]
+            cum_row = cum_ref[sub, head : head + 1]
             last = cum_row[:, SPAN - 1 : SPAN]
-            faded = split(keys_t[head // group] * jnp.exp(last - cum_row))
+            faded = split(turned_ref[sub * key_heads + head // group] * jnp.exp(last - cum_row))
             gathered = product(faded, solved)
             maps = unit * jnp.exp(last) - gathered[:, :DK]
-            map_ref[head] = beside(*split(maps))
-            add_ref[head] = gathered[:, DK:]
-
-    def one_round(span, carried):
-        before = jnp.maximum(span - 1, 0)
-        follow(before)
-        solve(before)
-        prepare(span)
+            map_ref[sub, head] = beside(*split(maps))
+            add_ref[sub, head] = gathered[:, DK:]
+
+    def one_round(group_at, carried):
+        follow(jnp.maximum(group_at - 2, 0))
+        solve(group_at - 1)
+        prepare(group_at)
         return carried
 
-    lax.fori_loop(0, spans, one_round, 0)
-    follow(spans - 1)
-    solve(spans - 1)
-    for head in range(heads):
-        fin_ref[head] = advance(head)
+    rounds = spans // GROUP
+    prepare(0)
+    lax.fori_loop(1, rounds, one_round, 0)
+    follow(rounds - 2)
+    solve(rounds - 1)
+    follow(rounds - 1)
     turn = turn_ref[0]
     for place, end_ref in enumerate((end0, end1, end2, end3)):
         end_ref[...] = fin_ref[lax.rem(turn + place, heads)]
@@ -466,19 +480,19 @@
             out_specs=[pl.BlockSpec(memory_space=pltpu.VMEM)] * 9,
             scratch_shapes=[
                 pltpu.VMEM((heads, 2, DK, 2 * DV), bf16),
-                pltpu.VMEM((heads, DK, 2 * DK), bf16),
-                pltpu.VMEM((heads, DK, DV), f32),
+                pltpu.VMEM((GROUP, heads, DK, 2 * DK), bf16),
+                pltpu.VMEM((GROUP, heads, DK, DV), f32),
                 pltpu.VMEM((heads, DK, 2 * DV), f32),
                 pltpu.VMEM((3, HALF, HALF), bf16),
                 pltpu.VMEM((2 * HALF, (BASE - 1) * HALF), bf16),
                 pltpu.VMEM((SPAN, SPAN), bf16),
-                pltpu.VMEM((2 * heads, 2, HALF, HALF), bf16),
-                pltpu.VMEM((heads, 2, HALF, HALF), bf16),
-                pltpu.VMEM((key_heads, SPAN, DK), f32),
-                pltpu.VMEM((key_heads, DK, SPAN), f32),
-                pltpu.VMEM((SPAN, value_width), f32),
-                pltpu.VMEM((SPAN, HALF), f32),
-                pltpu.VMEM((2 * heads, SPAN), f32),
+                pltpu.VMEM((2 * GROUP * heads, 2, HALF, HALF), bf16),
+                pltpu.VMEM((GROUP * heads, 2, HALF, HALF), bf16),
+                pltpu.VMEM((GROUP * key_heads, SPAN, DK), f32),
+                pltpu.VMEM((GROUP * key_heads, DK, SPAN), f32),
+                pltpu.VMEM((GROUP, SPAN, value_width), f32),
+                pltpu.VMEM((GROUP, SPAN, HALF), f32),
+                pltpu.VMEM((GROUP, 2 * heads, SPAN), f32),
             ],
         ),
         out_shape=[

time: 67.7 us -> 65.6 us (0.969)
  Pallas kernels: 41 us -> 38.7 us
    pallas_call x1, Pallas kernels: 27.8 us -> 25.6 us  [per_device(): pl.pallas_call(state_kernel, grid_spec=pltpu.PrefetchScalarGridSpec(num_s...]
  transfers between devices with their start and end apart: 10 -> 10, of which waited for: 5 -> 5; matrix products, arithmetic and copies ran while one was open for 0% -> 0% of each run, Pallas kernels for 12% -> 13%
where the time goes in v4:
time: 65.6 us; the launch traced here: 65.4 us
  Pallas kernels  38.7 us (59%)
  starting transfers between devices  22.2 us (34%)
  waiting for transfers between devices  4.09 us (6%)
    pallas_call x1, Pallas kernels, per_device(): pl.pallas_call(state_kernel, grid_spec=pltpu.PrefetchScalarGridSpec(num_s...  25.6 us
    ppermute x10, starting transfers between devices, shifted(): return lax.ppermute(value, axis, pairs)  22.2 us
    pallas_call x3, Pallas kernels, query_part(): pl.pallas_call(body, in_specs=[pl.BlockSpec(memory_space=pltpu.VMEM)] * (...  8.22 us
    ppermute x10, waiting for transfers between devices, shifted(): return lax.ppermute(value, axis, pairs)  4.09 us
    pallas_call x1, Pallas kernels, per_device(): pl.pallas_call(close_kernel, grid_spec=pltpu.PrefetchScalarGridSpec(num_s...  2.74 us
  transfers between devices with their start and end apart: 10, of which 5 were waited for; matrix products, arithmetic and copies ran while one was open for 0% of the time, Pallas kernels for 13%

profile of v4, /device:TPU:0, one launch (start us, length us, event | category | flops | bytes accessed | tf_op | source)
XLA Modules:
  0.0 65.4 jit_solution(11891137531015614258)
XLA Ops:
  0.0 0.0 copy-start.6
  0.0 0.9 %pack.1 = bf16[16,1024]{1,0:T(8,128)(2,1)S(1)} custom-call(bf16[2048,256]{1,0:T(8,128)(2,1)} %refs_0_.5, bf16[2048,256]{1,0:T(8,128)(2,1)} %key_ref.3, bf16[2048,512]{1,0:T(8,128)(2,1)} %val_ref.3), custom_call_target="tpu_custom_call" | custom-call | bytes 64000 | tf_op jit(solution)/shard_map/pack/pallas_call | solution.py:456
  0.9 3.7 %collective-permute-start = (bf16[16,1024]{1,0:T(8,128)(2,1)S(1)}, bf16[16,1024]{1,0:T(8,128)(2,1)S(1)}, u32[]{:S(2)}, u32[]{:S(2)}) collective-permute-start(bf16[16,1024]{1,0:T(8,128)(2,1)S(1)} %pack.1), channel_id=1, source_target_pairs={{0,1},{1,2},{2,3},{3,4},{4,5},{5,6},{6,7},{7,8},{8,9},{9,10},{10,1... | collective-permute-start | bytes 98312 | tf_op jit(solution)/shard_map/ppermute | solution.py:29
  4.7 1.5 %collective-permute-done.halo_ref.refs_1_ = bf16[16,1024]{1,0:T(8,128)(2,1)S(1)} collective-permute-done((bf16[16,1024]{1,0:T(8,128)(2,1)S(1)}, bf16[16,1024]{1,0:T(8,128)(2,1)S(1)}, u32[]{:S(2)}, u32[]{:S(2)}) %collective-permute-start) | collective-permute-done | bytes 32800 | tf_op jit(solution)/shard_map/ppermute | solution.py:29
  6.2 0.0 copy-start
  6.2 0.0 copy-start.3
  6.3 25.6 %state_path.1 = (bf16[8,2,2,128,256]{4,3,2,1,0:T(8,128)(2,1)S(1)}, bf16[8,4,2,256,256]{4,3,2,1,0:T(8,128)(2,1)S(1)}, bf16[8,4,2,128,256]{4,3,2,1,0:T(8,128)(2,1)...) custom-call(s32[1]{0:T(128)} %bitcast.turn_ref, ...), custom_call_target="tpu_custom_call" | custom-call | flops 20000000000 | bytes 20000000 | tf_op jit(solution)/shard_map/state_path/pallas_call | solution.py:474
  31.9 2.4 %collective-permute-start.1 = (f32[128,256]{1,0:T(8,128)S(1)}, f32[128,256]{1,0:T(8,128)S(1)}, u32[]{:S(2)}, u32[]{:S(2)}) collective-permute-start(f32[128,256]{1,0:T(8,128)S(1)} %get-tuple-element.37), channel_id=1, source_target_pairs={{0,1},{1,2},{2,3},{3,0},{4,5},{5,6},{6,7},{7,4},{8,9},{9,10},{10,1... | collective-permute-start | bytes 393224 | tf_op jit(solution)/shard_map/ppermute | solution.py:29
  34.3 2.9 %collective-permute-start.2 = (f32[128,256]{1,0:T(8,128)S(1)}, f32[128,256]{1,0:T(8,128)S(1)}, u32[]{:S(2)}, u32[]{:S(2)}) collective-permute-start(f32[128,256]{1,0:T(8,128)S(1)} %get-tuple-element.38), channel_id=1, source_target_pairs={{0,2},{1,3},{2,0},{3,1},{4,6},{5,7},{6,4},{7,5},{8,10},{9,11},{10,... | collective-permute-start | bytes 393224 | tf_op jit(solution)/shard_map/ppermute | solution.py:29
  37.2 1.3 %collective-permute-start.3 = (f32[128,256]{1,0:T(8,128)S(1)}, f32[128,256]{1,0:T(8,128)S(1)}, u32[]{:S(2)}, u32[]{:S(2)}) collective-permute-start(f32[128,256]{1,0:T(8,128)S(1)} %get-tuple-element.39), channel_id=1, source_target_pairs={{0,3},{1,0},{2,1},{3,2},{4,7},{5,4},{6,5},{7,6},{8,11},{9,8},{10,9... | collective-permute-start | bytes 393224 | tf_op jit(solution)/shard_map/ppermute | solution.py:29
  38.5 0.0 copy-done.3
  38.6 3.1 %query_path.3 = (f32[2048,512]{1,0:T(8,128)S(1)}, bf16[2048,1024]{1,0:T(8,128)(2,1)S(1)}) custom-call(bf16[2048,256]{1,0:T(8,128)(2,1)S(1)} %copy-done, bf16[16,1024]{1,0:T(8,128)(2,1)S(1)} %collective-permute-done.halo_ref.refs_1_, bf16[4,256]{1,0:T(4,128)(2,1)S(1)} %copy-done.3, bf16[8,2,2,128,256]{4,3,2,1,0:T(8,128)(2,1)S(1)} %get-tuple-element.40.refs_3_, ...), custom_call_target="tpu_custom_call" | custom-call | flops 6000000000 | bytes 9000000 | tf_op jit(solution)/shard_map/query_path/pallas_call | solution.py:522
  41.6 0.0 collective-permute-done.1.part1
  41.6 0.5 collective-permute-done.2.part2
  42.1 0.1 collective-permute-done.3.part3
  42.2 0.6 compose.1
  42.8 4.6 %collective-permute-start.5 = (f32[128,256]{1,0:T(8,128)S(1)}, f32[128,256]{1,0:T(8,128)S(1)}, u32[]{:S(2)}, u32[]{:S(2)}) collective-permute-start(f32[128,256]{1,0:T(8,128)S(1)} %get-tuple-element.51), channel_id=1, source_target_pairs={{0,8},{4,12},{8,0},{12,4},{1,9},{5,13},{9,1},{13,5},{2,10},{6,14},... | collective-permute-start | bytes 393224 | tf_op jit(solution)/shard_map/ppermute | solution.py:29
  47.3 0.6 collective-permute-start.4
  47.9 2.7 %collective-permute-start.6 = (f32[128,128]{1,0:T(8,128)S(1)}, f32[128,128]{1,0:T(8,128)S(1)}, u32[]{:S(2)}, u32[]{:S(2)}) collective-permute-start(f32[128,128]{1,0:T(8,128)S(1)} %get-tuple-element.57), channel_id=1, source_target_pairs={{0,12},{4,0},{8,4},{12,8},{1,13},{5,1},{9,5},{13,9},{2,14},{6,2},{... | collective-permute-start | bytes 196616 | tf_op jit(solution)/shard_map/ppermute | solution.py:29
  50.6 2.1 %query_path.4 = (f32[2048,512]{1,0:T(8,128)S(1)}, bf16[2048,1024]{1,0:T(8,128)(2,1)S(1)}) custom-call(bf16[2048,256]{1,0:T(8,128)(2,1)S(1)} %copy-done, bf16[16,1024]{1,0:T(8,128)(2,1)S(1)} %collective-permute-done.halo_ref.refs_1_, bf16[4,256]{1,0:T(4,128)(2,1)S(1)} %copy-done.3, ...), custom_call_target="tpu_custom_call", output_to_operand_aliasing={{0}: (8, {}), {1}: (9, {})} | custom-call | flops 4000000000 | bytes 6000000 | tf_op jit(solution)/shard_map/query_path/pallas_call | solution.py:522
  52.7 0.8 %collective-permute-done.4.near_ref = f32[128,256]{1,0:T(8,128)S(1)} collective-permute-done((f32[128,256]{1,0:T(8,128)S(1)}, f32[128,256]{1,0:T(8,128)S(1)}, u32[]{:S(2)}, u32[]{:S(2)}) %collective-permute-start.4) | collective-permute-done | bytes 131104 | tf_op jit(solution)/shard_map/ppermute | solution.py:29
  53.5 0.0 collective-permute-done.6.far_ref
  53.5 0.0 collective-permute-done.5.next_ref
  53.5 0.6 enter.1
  54.2 0.5 collective-permute-start.7
  54.6 3.6 %collective-permute-start.8 = (f32[128,128]{1,0:T(8,128)S(1)}, f32[128,128]{1,0:T(8,128)S(1)}, u32[]{:S(2)}, u32[]{:S(2)}) collective-permute-start(f32[128,128]{1,0:T(8,128)S(1)} %get-tuple-element.61), channel_id=1, source_target_pairs={{0,2},{1,3},{2,0},{3,1},{4,6},{5,7},{6,4},{7,5},{8,10},{9,11},{10,... | collective-permute-start | bytes 196616 | tf_op jit(solution)/shard_map/ppermute | solution.py:29
  58.2 0.0 collective-permute-start.9
  58.2 3.1 %query_path.5 = (f32[2048,512]{1,0:T(8,128)S(1)}, bf16[2048,1024]{1,0:T(8,128)(2,1)S(1)}) custom-call(bf16[2048,256]{1,0:T(8,128)(2,1)S(1)} %copy-done, bf16[16,1024]{1,0:T(8,128)(2,1)S(1)} %collective-permute-done.halo_ref.refs_1_, bf16[4,256]{1,0:T(4,128)(2,1)S(1)} %copy-done.3, ...), custom_call_target="tpu_custom_call", output_to_operand_aliasing={{0}: (8, {}), {1}: (9, {})} | custom-call | flops 6000000000 | bytes 9000000 | tf_op jit(solution)/shard_map/query_path/pallas_call | solution.py:522
  61.2 0.0 collective-permute-done.7.part1
  61.3 0.0 collective-permute-done.8.part2
  61.3 1.2 %collective-permute-done.9.part3 = f32[128,128]{1,0:T(8,128)S(1)} collective-permute-done((f32[128,128]{1,0:T(8,128)S(1)}, f32[128,128]{1,0:T(8,128)S(1)}, u32[]{:S(2)}, u32[]{:S(2)}) %collective-permute-start.9) | collective-permute-done | bytes 65568 | tf_op jit(solution)/shard_map/ppermute | solution.py:29
  62.4 2.7 %close.1 = bf16[2048,512]{1,0:T(8,128)(2,1)} custom-call(s32[1]{0:T(128)} %bitcast.turn_ref, f32[128,128]{1,0:T(8,128)S(1)} %get-tuple-element.59.part0, f32[128,128]{1,0:T(8,128)S(1)} %collective-permute-done.7.part1, f32[128,128]{1,0:T(8,128)S(1)} %collective-permute-done.8.part2, f32[128,128]{1,0:T(8,128)S(1)} %collective-permute-done.9.part3, ...), custom_call_target="tpu_custom_call" | custom-call | flops 2000000000 | bytes 10000000 | tf_op jit(solution)/shard_map/close/pallas_call | solution.py:579
  (15 shorter events, 0.0 us)
Async XLA Ops:
  0.0 6.2 %copy-start.1 = (bf16[2048,512]{1,0:T(8,128)(2,1)S(1)}, bf16[2048,512]{1,0:T(8,128)(2,1)}, u32[]{:S(2)}) copy-start(bf16[2048,512]{1,0:T(8,128)(2,1)} %val_ref.3) | copy-start | bytes 6291460
  0.0 6.2 %copy-start.2 = (bf16[2048,256]{1,0:T(8,128)(2,1)S(1)}, bf16[2048,256]{1,0:T(8,128)(2,1)}, u32[]{:S(2)}) copy-start(bf16[2048,256]{1,0:T(8,128)(2,1)} %key_ref.3) | copy-start | bytes 3145732
  0.0 4.6 %copy-start.7 = (f32[2048,4]{0,1:T(4,128)S(1)}, f32[2048,4]{0,1:T(4,128)}, u32[]{:S(2)}) copy-start(f32[2048,4]{0,1:T(4,128)} %param.13) | copy-start | bytes 98308
  0.0 4.6 %copy-start.8 = (f32[2048,4]{0,1:T(4,128)S(1)}, f32[2048,4]{0,1:T(4,128)}, u32[]{:S(2)}) copy-start(f32[2048,4]{0,1:T(4,128)} %param.12) | copy-start | bytes 98308
  0.0 6.2 %copy-start.5 = (bf16[4,512]{1,0:T(4,128)(2,1)S(1)}, bf16[4,512]{1,0:T(4,128)(2,1)}, u32[]{:S(2)}) copy-start(bf16[4,512]{1,0:T(4,128)(2,1)} %val_taps.1) | copy-start | bytes 12292
  0.0 6.2 %copy-start.6 = (bf16[4,256]{1,0:T(4,128)(2,1)S(1)}, bf16[4,256]{1,0:T(4,128)(2,1)}, u32[]{:S(2)}) copy-start(bf16[4,256]{1,0:T(4,128)(2,1)} %key_taps.1) | copy-start | bytes 6148
  0.9 5.3 %collective-permute-start = (bf16[16,1024]{1,0:T(8,128)(2,1)S(1)}, bf16[16,1024]{1,0:T(8,128)(2,1)S(1)}, u32[]{:S(2)}, u32[]{:S(2)}) collective-permute-start(bf16[16,1024]{1,0:T(8,128)(2,1)S(1)} %pack.1), channel_id=1, source_target_pairs={{0,1},{1,2},{2,3},{3,4},{4,5},{5,6},{6,7},{7,8},{8,9},{9,10},{10,1... | collective-permute-start | bytes 98312 | tf_op jit(solution)/shard_map/ppermute | solution.py:29
  6.2 32.3 %copy-start = (bf16[2048,256]{1,0:T(8,128)(2,1)S(1)}, bf16[2048,256]{1,0:T(8,128)(2,1)}, u32[]{:S(2)}) copy-start(bf16[2048,256]{1,0:T(8,128)(2,1)} %refs_0_.5) | copy-start | bytes 3145732
  6.2 32.3 %copy-start.3 = (bf16[4,256]{1,0:T(4,128)(2,1)S(1)}, bf16[4,256]{1,0:T(4,128)(2,1)}, u32[]{:S(2)}) copy-start(bf16[4,256]{1,0:T(4,128)(2,1)} %refs_2_.5) | copy-start | bytes 6148
  31.9 9.7 %collective-permute-start.1 = (f32[128,256]{1,0:T(8,128)S(1)}, f32[128,256]{1,0:T(8,128)S(1)}, u32[]{:S(2)}, u32[]{:S(2)}) collective-permute-start(f32[128,256]{1,0:T(8,128)S(1)} %get-tuple-element.37), channel_id=1, source_target_pairs={{0,1},{1,2},{2,3},{3,0},{4,5},{5,6},{6,7},{7,4},{8,9},{9,10},{10,1... | collective-permute-start | bytes 393224 | tf_op jit(solution)/shard_map/ppermute | solution.py:29
  34.3 7.8 %collective-permute-start.2 = (f32[128,256]{1,0:T(8,128)S(1)}, f32[128,256]{1,0:T(8,128)S(1)}, u32[]{:S(2)}, u32[]{:S(2)}) collective-permute-start(f32[128,256]{1,0:T(8,128)S(1)} %get-tuple-element.38), channel_id=1, source_target_pairs={{0,2},{1,3},{2,0},{3,1},{4,6},{5,7},{6,4},{7,5},{8,10},{9,11},{10,... | collective-permute-start | bytes 393224 | tf_op jit(solution)/shard_map/ppermute | solution.py:29
  37.2 5.0 %collective-permute-start.3 = (f32[128,256]{1,0:T(8,128)S(1)}, f32[128,256]{1,0:T(8,128)S(1)}, u32[]{:S(2)}, u32[]{:S(2)}) collective-permute-start(f32[128,256]{1,0:T(8,128)S(1)} %get-tuple-element.39), channel_id=1, source_target_pairs={{0,3},{1,0},{2,1},{3,2},{4,7},{5,4},{6,5},{7,6},{8,11},{9,8},{10,9... | collective-permute-start | bytes 393224 | tf_op jit(solution)/shard_map/ppermute | solution.py:29
  42.8 10.7 %collective-permute-start.5 = (f32[128,256]{1,0:T(8,128)S(1)}, f32[128,256]{1,0:T(8,128)S(1)}, u32[]{:S(2)}, u32[]{:S(2)}) collective-permute-start(f32[128,256]{1,0:T(8,128)S(1)} %get-tuple-element.51), channel_id=1, source_target_pairs={{0,8},{4,12},{8,0},{12,4},{1,9},{5,13},{9,1},{13,5},{2,10},{6,14},... | collective-permute-start | bytes 393224 | tf_op jit(solution)/shard_map/ppermute | solution.py:29
  47.3 6.2 %collective-permute-start.4 = (f32[128,256]{1,0:T(8,128)S(1)}, f32[128,256]{1,0:T(8,128)S(1)}, u32[]{:S(2)}, u32[]{:S(2)}) collective-permute-start(f32[128,256]{1,0:T(8,128)S(1)} %get-tuple-element.51), channel_id=1, source_target_pairs={{0,4},{4,8},{8,12},{12,0},{1,5},{5,9},{9,13},{13,1},{2,6},{6,10},{... | collective-permute-start | bytes 393224 | tf_op jit(solution)/shard_map/ppermute | solution.py:29
  47.9 5.6 %collective-permute-start.6 = (f32[128,128]{1,0:T(8,128)S(1)}, f32[128,128]{1,0:T(8,128)S(1)}, u32[]{:S(2)}, u32[]{:S(2)}) collective-permute-start(f32[128,128]{1,0:T(8,128)S(1)} %get-tuple-element.57), channel_id=1, source_target_pairs={{0,12},{4,0},{8,4},{12,8},{1,13},{5,1},{9,5},{13,9},{2,14},{6,2},{... | collective-permute-start | bytes 196616 | tf_op jit(solution)/shard_map/ppermute | solution.py:29
  54.2 7.1 %collective-permute-start.7 = (f32[128,128]{1,0:T(8,128)S(1)}, f32[128,128]{1,0:T(8,128)S(1)}, u32[]{:S(2)}, u32[]{:S(2)}) collective-permute-start(f32[128,128]{1,0:T(8,128)S(1)} %get-tuple-element.60), channel_id=1, source_target_pairs={{0,1},{1,2},{2,3},{3,0},{4,5},{5,6},{6,7},{7,4},{8,9},{9,10},{10,1... | collective-permute-start | bytes 196616 | tf_op jit(solution)/shard_map/ppermute | solution.py:29
  54.6 6.7 %collective-permute-start.8 = (f32[128,128]{1,0:T(8,128)S(1)}, f32[128,128]{1,0:T(8,128)S(1)}, u32[]{:S(2)}, u32[]{:S(2)}) collective-permute-start(f32[128,128]{1,0:T(8,128)S(1)} %get-tuple-element.61), channel_id=1, source_target_pairs={{0,2},{1,3},{2,0},{3,1},{4,6},{5,7},{6,4},{7,5},{8,10},{9,11},{10,... | collective-permute-start | bytes 196616 | tf_op jit(solution)/shard_map/ppermute | solution.py:29
  58.2 4.3 %copy-start.4 = (f32[512]{0:T(512)S(1)}, f32[512]{0:T(512)}, u32[]{:S(2)}) copy-start(f32[512]{0:T(512)} %param.17) | copy-start | bytes 6148
  58.2 4.3 %collective-permute-start.9 = (f32[128,128]{1,0:T(8,128)S(1)}, f32[128,128]{1,0:T(8,128)S(1)}, u32[]{:S(2)}, u32[]{:S(2)}) collective-permute-start(f32[128,128]{1,0:T(8,128)S(1)} %get-tuple-element.62), channel_id=1, source_target_pairs={{0,3},{1,0},{2,1},{3,2},{4,7},{5,4},{6,5},{7,6},{8,11},{9,8},{10,9... | collective-permute-start | bytes 196616 | tf_op jit(solution)/shard_map/ppermute | solution.py:29
